TPU v7x, 256 devices: a whole 4x4x8 slice. The times are simulated.
256 devices in a mesh: blk: 64 (over z, y, core), rep: 4 (over x).
Axes of the slice: x: 4, y: 4, z: 8, core: 2. Of those that a mesh axis runs over, the one named last changes fastest.
Arguments:
- blocks: bfloat16 [1024, 128, 8192], P(('blk', 'rep')), may hold values from -6 to 6
- coords: int32 [3, 1024], P(None, ('blk', 'rep')), may hold values from 0 to 2047, as said below
- counts: int32 [256], P(('blk', 'rep')), may hold values from 1 to 4, as said below
- factor_b: bfloat16 [131072, 32], P('blk'), may hold values from -2 to 2
- factor_c: bfloat16 [32768, 16], P('blk'), may hold values from -3 to 3
- start: float32 [512, 32], replicated, may hold values from -6 to 6
Outputs:
- factor_a: float32 [262144, 32], P(('blk', 'rep'))
Inputs may be any that keep to these rules, and one draw needn't show every extreme that they name: coords[0] of a slot on blk index b lies in b * 32 to (b + 1) * 32 - 1; coords[1] lies below 1024 and coords[2] below 512. Among the 4 slots of one device, at most 2 have coords[1] in the same slab of 16 row blocks, and at most 2 have coords[2] in the same slab of 8 row blocks; every device reaches both bounds. Slots 0 to counts - 1 of a device hold live blocks; some device has all 4 live.
All inputs are finite; a program needn't handle non-finite values.
Results may differ from a plain program's by a relative error of at most 0.003.
Values may be sent and summed in bfloat16 or wider, within the bound.
A program may use at most 128 MiB of HBM per device.

v0:
```python
import jax
import jax.numpy as jnp
from jax import lax
from jax.sharding import PartitionSpec as P

BI = 128
BJ = 128
BK = 64
R2 = 32
R3 = 16
RR = 512
IB_DEV = 32
ITERS = 4


def orthonormal(matrix):
    inner = jnp.dot(matrix.T, matrix, precision=lax.Precision.HIGHEST)
    lower_factor = jnp.linalg.cholesky(inner)
    return jax.scipy.linalg.solve_triangular(lower_factor, matrix.T, lower=True).T


def route_rows(global_id, per_owner, groups, capacity):
    owner_of = global_id // per_owner
    local_id = global_id % per_owner
    slot_range = jnp.arange(global_id.shape[0], dtype=jnp.int32)
    earlier = (owner_of[:, None] == owner_of[None, :]) & (slot_range[:, None] > slot_range[None, :])
    rank_in = jnp.sum(earlier.astype(jnp.int32), axis=1)
    chosen = (owner_of[:, None, None] == jnp.arange(groups, dtype=jnp.int32)[None, :, None]) & (
        rank_in[:, None, None] == jnp.arange(capacity, dtype=jnp.int32)[None, None, :]
    )
    request_table = jnp.sum(jnp.where(chosen, local_id[:, None, None], 0), axis=0)
    return (owner_of, rank_in, request_table)


def place_rows(count, block_ids, weights, contributions):
    rows_here = jnp.arange(count, dtype=jnp.int32)
    block_here = rows_here // BI
    within = rows_here % BI
    selector = (block_ids[None, :, None] == block_here[:, None, None]) & (
        jnp.arange(BI, dtype=jnp.int32)[None, None, :] == within[:, None, None]
    )
    placing = selector.astype(jnp.float32) * weights[None, :, None]
    return jnp.dot(
        placing.reshape(count, block_ids.shape[0] * BI),
        contributions,
        precision=lax.Precision.HIGHEST,
    )


def body(blocks, coords, counts, factor_b, factor_c, start):
    groups = lax.axis_size("blk")
    slot_count = blocks.shape[0]
    capacity = min(2, slot_count)
    slab_b = factor_b.reshape(-1, BJ * R2)
    slab_c = factor_c.reshape(-1, BK * R3)
    positions = jnp.arange(slot_count, dtype=jnp.int32)
    alive = (positions < counts[0]).astype(jnp.float32)
    owner_b, rank_b, request_b = route_rows(coords[1], slab_b.shape[0], groups, capacity)
    owner_c, rank_c, request_c = route_rows(coords[2], slab_c.shape[0], groups, capacity)
    asked_b = lax.all_to_all(request_b, "blk", split_axis=0, concat_axis=0, tiled=True)
    asked_c = lax.all_to_all(request_c, "blk", split_axis=0, concat_axis=0, tiled=True)
    fetched_b = lax.all_to_all(slab_b[asked_b], "blk", split_axis=0, concat_axis=0, tiled=True)
    fetched_c = lax.all_to_all(slab_c[asked_c], "blk", split_axis=0, concat_axis=0, tiled=True)
    picked_c = fetched_c[owner_c, rank_c]
    picked_b = fetched_b[owner_b, rank_b]
    cube = blocks.reshape(slot_count, BI, BJ, BK)
    folded = jnp.einsum(
        "sijk,skr->sirj",
        cube,
        picked_c.reshape(slot_count, BK, R3),
        preferred_element_type=jnp.float32,
    ).astype(jnp.bfloat16)
    partial_rows = jnp.einsum(
        "sirj,sjq->siqr",
        folded,
        picked_b.reshape(slot_count, BJ, R2),
        preferred_element_type=jnp.float32,
    )
    partial_rows = partial_rows.reshape(slot_count * BI, RR)
    local_block = coords[0] % IB_DEV
    row_share = IB_DEV * BI // lax.axis_size("rep")
    unfolded = lax.psum_scatter(
        place_rows(row_share * lax.axis_size("rep"), local_block, alive, partial_rows),
        "rep",
        scatter_dimension=0,
        tiled=True,
    )
    gram_matrix = lax.psum(
        jnp.dot(unfolded.T, unfolded, precision=lax.Precision.HIGHEST), ("blk", "rep")
    )
    subspace = orthonormal(start)
    for iteration in range(ITERS):
        subspace = orthonormal(jnp.dot(gram_matrix, subspace, precision=lax.Precision.HIGHEST))
    mapped = jnp.dot(unfolded, subspace, precision=lax.Precision.HIGHEST)
    small_gram = lax.psum(
        jnp.dot(mapped.T, mapped, precision=lax.Precision.HIGHEST), ("blk", "rep")
    )
    lower_factor = jnp.linalg.cholesky(small_gram)
    return jax.scipy.linalg.solve_triangular(lower_factor, mapped.T, lower=True).T


def solution(mesh):
    return jax.shard_map(
        body,
        mesh=mesh,
        in_specs=(
            P(("blk", "rep"), None, None),
            P(None, ("blk", "rep")),
            P(("blk", "rep")),
            P("blk", None),
            P("blk", None),
            P(),
        ),
        out_specs=P(("blk", "rep"), None),
        check_vma=False,
    )
```

profile of v0, /device:TPU:1, one launch (start us, length us, event | category | flops | bytes accessed | tf_op | source)
XLA Modules:
  0.0 612.7 jit_solution(2463133279720920973)
XLA Ops:
  9.2 13.2 %all-to-all-start.2 = ((s32[64,1,2]{2,1,0:T(1,128)}), s32[64,1,2]{2,1,0:T(1,128)S(1)}, u32[]{:S(2)}, u32[]{:S(2)}) async-start(s32[64,1,2]{2,1,0:T(1,128)} %copy.60), calls=%async_computation.2 | async-start | bytes 65536 | tf_op jit(solution)/shard_map/all_to_all | solution.py:61
  22.4 1.9 iota_compare_fusion
  26.1 5.6 all-to-all-done.2
  31.7 4.7 all-to-all-start
  38.5 7.5 %all-to-all-done = s32[64,1,2]{2,1,0:T(1,128)S(1)} async-done(((s32[64,1,2]{2,1,0:T(1,128)}), s32[64,1,2]{2,1,0:T(1,128)S(1)}, u32[]{:S(2)}, u32[]{:S(2)}) %all-to-all-start) | async-done | bytes 544 | tf_op jit(solution)/shard_map/all_to_all | solution.py:60
  45.9 4.7 all-to-all-start.3
  50.7 11.9 %copy.63 = bf16[4,128,8192]{1,2,0:T(8,128)(2,1)} copy(bf16[4,128,8192]{2,1,0:T(8,128)(2,1)} %param.9) | data formatting | bytes 16777216 | tf_op args[0]
  62.7 13.6 %copy.65 = bf16[4,128,128,64]{2,3,1,0:T(8,128)(2,1)} copy(bf16[4,128,128,64]{1,3,2,0:T(8,128)(2,1)} %bitcast.200) | data formatting | bytes 16777216 | tf_op jit(solution)/shard_map/reshape | solution.py:66
  82.4 10.4 %all-to-all-start.1 = ((bf16[64,2,4096]{2,1,0:T(2,128)(2,1)}), bf16[64,2,4096]{2,1,0:T(2,128)(2,1)S(1)}, u32[]{:S(2)}, u32[]{:S(2)}) async-start(bf16[64,2,4096]{2,1,0:T(2,128)(2,1)} %reshape.626), calls=%async_computation.1 | async-start | bytes 2097152 | tf_op jit(solution)/shard_map/all_to_all | solution.py:62
  93.0 18.4 %and_select_fusion = f32[4096,4,128]{2,1,0:T(4,128)} fusion(f32[4]{0:T(128)S(1)} %compare_convert_fusion, pred[4096,128]{1,0:T(8,128)(4,1)S(1)} %iota_compare_fusion, pred[4096,4]{1,0:T(8,128)(4,1)S(1)} %copy.54), kind=kLoop, calls=%fused_computation.7 | loop fusion | flops 4194304 | bytes 8929296 | tf_op jit(solution)/shard_map/mul | solution.py:42
  111.4 1.5 gather_fusion.3
  113.1 4.6 convert_bitcast_fusion
  117.7 3.1 all-to-all-done.1
  123.1 18.0 %fusion = f32[4096,512]{1,0:T(8,128)} fusion(f32[512,8,4,128]{3,2,1,0:T(4,128)} %bitcast.199, f32[64,8,4,128]{3,2,1,0:T(4,128)S(1)} %bitcast.201), kind=kOutput, calls=%fused_computation.4 | convolution fusion | flops 12884901888 | bytes 17825792 | tf_op jit(solution)/shard_map/dot_general | solution.py:43
  141.7 2.9 cholesky.104
  144.6 77.7 %reduce-scatter.2.cloned.1.call-done = f32[1024,512]{1,0:T(8,128)} async-done(((f32[4096,512]{1,0:T(8,128)}), f32[1024,512]{1,0:T(8,128)}) %reduce-scatter.2.cloned.1.call-update) | async-done | bytes 2097168 | tf_op jit(solution)/shard_map/reduce_scatter | solution.py:82
  222.3 6.8 %fusion.73 = f32[512,512]{1,0:T(8,128)} fusion(f32[1024,512]{1,0:T(8,128)} %reduce-scatter.2.cloned.1.call-done), kind=kOutput, calls=%fused_computation.156 | convolution fusion | flops 3221225472 | bytes 3145728 | tf_op jit(solution)/shard_map/dot_general | solution.py:89
  230.4 2.4 custom-call.18
  233.1 250.3 %all-reduce.2.cloned.1.call-done = f32[512,512]{1,0:T(8,128)} async-done(((f32[512,512]{1,0:T(8,128)}), f32[512,512]{1,0:T(8,128)}) %all-reduce.2.cloned.1.call-update) | async-done | bytes 1048592 | tf_op jit(solution)/shard_map/psum | solution.py:88
  483.5 2.4 fusion.75
  486.1 2.9 cholesky.115
  490.4 2.4 custom-call.19
  494.5 2.9 cholesky.126
  498.7 2.4 custom-call.20
  502.8 2.9 cholesky.137
  507.1 2.4 custom-call.21
  511.2 2.9 cholesky.148
  515.4 2.4 custom-call.22
  518.2 2.0 fusion.83
  520.4 77.6 %psum.15 = f32[32,32]{0,1:T(8,128)S(1)} all-reduce(f32[32,32]{0,1:T(8,128)S(1)} %fusion.84), channel_id=1, replica_groups=mesh['blk'=64,'rep'=4] {'blk','rep'}, use_global_device_ids=true, to_apply=%region_8.11 | all-reduce | flops 1024 | bytes 8192 | tf_op jit(solution)/shard_map/psum | solution.py:95
  598.2 2.9 cholesky.159
  602.4 2.4 custom-call.9
  (102 shorter events, 30.2 us)
Async XLA Ops:
  6.5 134.8 %copy-start = (f32[512,32]{0,1:T(8,128)S(1)}, f32[512,32]{0,1:T(8,128)}, u32[]{:S(2)}) copy-start(f32[512,32]{0,1:T(8,128)} %param.14) | copy-start | bytes 196612
  9.2 22.5 %all-to-all-start.2 = ((s32[64,1,2]{2,1,0:T(1,128)}), s32[64,1,2]{2,1,0:T(1,128)S(1)}, u32[]{:S(2)}, u32[]{:S(2)}) async-start(s32[64,1,2]{2,1,0:T(1,128)} %copy.60), calls=%async_computation.2 | async-start | bytes 65536 | tf_op jit(solution)/shard_map/all_to_all | solution.py:61
  31.7 14.2 %all-to-all-start = ((s32[64,1,2]{2,1,0:T(1,128)}), s32[64,1,2]{2,1,0:T(1,128)S(1)}, u32[]{:S(2)}, u32[]{:S(2)}) async-start(s32[64,1,2]{2,1,0:T(1,128)} %copy.56), calls=%async_computation | async-start | bytes 65536 | tf_op jit(solution)/shard_map/all_to_all | solution.py:60
  45.9 35.7 %all-to-all-start.3 = ((bf16[64,2,1024]{2,1,0:T(2,128)(2,1)}), bf16[64,2,1024]{2,1,0:T(2,128)(2,1)S(1)}, u32[]{:S(2)}, u32[]{:S(2)}) async-start(bf16[64,2,1024]{2,1,0:T(2,128)(2,1)} %reshape.640), calls=%async_computation.3 | async-start | bytes 524288 | tf_op jit(solution)/shard_map/all_to_all | solution.py:63
  62.7 13.6 %copy-start.4 = (bf16[2048,32]{0,1:T(8,128)(2,1)S(1)}, bf16[2048,32]{0,1:T(8,128)(2,1)}, u32[]{:S(2)}) copy-start(bf16[2048,32]{0,1:T(8,128)(2,1)} %param.12) | copy-start | bytes 393220
  80.1 12.9 %copy-start.5 = (s32[3,4]{1,0:T(4,128)S(1)}, s32[3,4]{1,0:T(4,128)}, u32[]{:S(2)}) copy-start(s32[3,4]{1,0:T(4,128)} %param.10) | copy-start | bytes 148
  81.6 0.7 copy-start.3
  82.4 38.4 %all-to-all-start.1 = ((bf16[64,2,4096]{2,1,0:T(2,128)(2,1)}), bf16[64,2,4096]{2,1,0:T(2,128)(2,1)S(1)}, u32[]{:S(2)}, u32[]{:S(2)}) async-start(bf16[64,2,4096]{2,1,0:T(2,128)(2,1)} %reshape.626), calls=%async_computation.1 | async-start | bytes 2097152 | tf_op jit(solution)/shard_map/all_to_all | solution.py:62
  92.8 129.5 %reduce-scatter.2.cloned.1.call-start = ((), (), s32[]{:S(2)}) async-start(), calls=%async_computation.5 | async-start | bytes 10485760 | tf_op jit(solution)/shard_map/reduce_scatter | solution.py:82
  141.1 342.4 %all-reduce.2.cloned.1.call-start = ((), (), s32[]{:S(2)}) async-start(), calls=%async_computation.6 | async-start | bytes 2097152 | tf_op jit(solution)/shard_map/psum | solution.py:88
  483.5 9.6 %copy-start.2 = (f32[512,512]{1,0:T(8,128)S(1)}, f32[512,512]{1,0:T(8,128)}, u32[]{:S(2)}) copy-start(f32[512,512]{1,0:T(8,128)} %all-reduce.2.cloned.1.call-done) | copy-start | bytes 3145732
  494.2 23.9 %copy-start.1 = (f32[1024,512]{1,0:T(8,128)S(1)}, f32[1024,512]{1,0:T(8,128)}, u32[]{:S(2)}) copy-start(f32[1024,512]{1,0:T(8,128)} %reduce-scatter.2.cloned.1.call-done) | copy-start | bytes 6291460
Sparse Core Ops, SparseCore 0:
  141.2 81.0 reduce-scatter.1
  229.2 254.1 all-reduce.1
where the time goes:
time: 614 us; the launch traced here: 613 us
  waiting for transfers between devices  344 us (56%)
  blocking collectives  77.6 us (13%)
  other arithmetic  62.6 us (10%)
  matrix products  41.5 us (7%)
  local copies, waits for them, and re-layouts  38.9 us (6%)
  starting transfers between devices  33.5 us (5%)
  between operations  14.5 us (2%)
    psum x1, waiting for transfers between devices, body(): lax.psum(jnp.dot(unfolded.T, unfolded, precision=lax.Precision.HIGHEST),...  250 us
    reduce_scatter x1, waiting for transfers between devices, body(): lax.psum_scatter(place_rows(row_share * lax.axis_size('rep'), local_block...  77.7 us
    psum x1, blocking collectives, body(): lax.psum(jnp.dot(mapped.T, mapped, precision=lax.Precision.HIGHEST), ('bl...  77.6 us
    mul x1, other arithmetic, place_rows(): placing = selector.astype(jnp.float32) * weights[None, :, None]  18.4 us
    dot_general x1, matrix products, place_rows(): jnp.dot(placing.reshape(count, block_ids.shape[0] * BI), contributions, p...  18 us
    another operation x15, other arithmetic, orthonormal(): lower_factor = jnp.linalg.cholesky(inner)  18 us
    another operation x10, other arithmetic, orthonormal(): jax.scipy.linalg.solve_triangular(lower_factor, matrix.T, lower=True)  15.4 us
    unnamed x15, local copies, waits for them, and re-layouts  13.8 us
  transfers between devices with their start and end apart: 6, of which 5 were waited for; matrix products, arithmetic and copies ran while one was open for 11% of the time, Pallas kernels for 0%

commit v1 on v0

v1 whole, which is shorter than its diff:
```python
import jax
import jax.numpy as jnp
from jax import lax
from jax.experimental import pallas as pl
from jax.experimental.pallas import tpu as pltpu
from jax.sharding import PartitionSpec as P

BI = 128
BJ = 128
BK = 64
R2 = 32
R3 = 16
RR = 512
IB_DEV = 32
ITERS = 4
NX = 4
NY = 4
NZ = 8
PACKED = 1280
HALF = PACKED // 2
PART_X = HALF // NX
PART_Y = PART_X // NY
HIGHEST = lax.Precision.HIGHEST
F32 = jnp.float32
BF16 = jnp.bfloat16
TILES = [(a, b) for a in range(4) for b in range(a, 4)]


def dot_nt(left, right):
    return lax.dot_general(left, right, (((1,), (1,)), ((), ())), preferred_element_type=F32)


def dot_tn(left, right):
    return lax.dot_general(left, right, (((0,), (0,)), ((), ())), preferred_element_type=F32)


def iota(shape, dim):
    return lax.broadcasted_iota(jnp.int32, shape, dim)


def contract_kernel(pick_ref, x_ref, c_ref, b_ref, p_ref, pb_ref):
    slot = pl.program_id(0)
    alive = (slot < pick_ref[5, 0]).astype(F32)
    odd = pick_ref[4, slot] > 0
    pair = c_ref[0, 0].astype(F32)
    mode_c = jnp.where(odd, pair[:, BK:], pair[:, :BK])
    wide = jnp.concatenate([mode_c] * 8, axis=1)
    tall = jnp.concatenate([wide] * 8, axis=0)
    fold_mask = iota((128, 512), 0) // R3 == iota((128, 512), 1) // BK
    fold_t = jnp.where(fold_mask, tall, 0.0).astype(BF16)
    spread_q = (iota((RR, R2), 0) // R3 == iota((RR, R2), 1)).astype(F32).astype(BF16)
    mode_b = jnp.dot(spread_q, b_ref[0, 0], preferred_element_type=F32).astype(BF16)
    keep = (iota((RR, 256), 0) % R3 == iota((RR, 256), 1) % R3).astype(F32)
    total = jnp.zeros((BI, RR), F32)
    for t in range(8):
        folded = jnp.concatenate(
            [
                dot_nt(x_ref[0, :, pl.ds((2 * t + h) * 512, 512)], fold_t).astype(BF16)
                for h in range(2)
            ],
            axis=1,
        )
        spread_j = (iota((BJ, 256), 0) == 16 * t + iota((BJ, 256), 1) // R3).astype(F32).astype(BF16)
        expanded = jnp.dot(mode_b, spread_j, preferred_element_type=F32) * keep
        total += dot_nt(folded, expanded.astype(BF16))
    total = total * alive
    p_ref[0] = total
    pb_ref[0] = total.astype(BF16)


def contract(blocks, picks, fetched):
    slots = blocks.shape[0]
    return pl.pallas_call(
        contract_kernel,
        grid_spec=pltpu.PrefetchScalarGridSpec(
            num_scalar_prefetch=1,
            grid=(slots,),
            in_specs=[
                pl.BlockSpec((1, BI, BJ * BK), lambda s, pick: (s, 0, 0)),
                pl.BlockSpec((1, 1, R3, 128), lambda s, pick: (pick[2, s], pick[3, s], 2, 0)),
                pl.BlockSpec((1, 1, R2, 128), lambda s, pick: (pick[0, s], pick[1, s], 0, 0)),
            ],
            out_specs=[
                pl.BlockSpec((1, BI, RR), lambda s, pick: (s, 0, 0)),
                pl.BlockSpec((1, BI, RR), lambda s, pick: (s, 0, 0)),
            ],
        ),
        out_shape=[
            jax.ShapeDtypeStruct((slots, BI, RR), F32),
            jax.ShapeDtypeStruct((slots, BI, RR), BF16),
        ],
        compiler_params=pltpu.CompilerParams(vmem_limit_bytes=40 * 1024 * 1024),
        name="contract",
    )(picks, blocks, fetched, fetched)


def gram_kernel(pb_ref, code_ref, gram_ref, rows, codes, g, o, from_c, from_x, from_y, from_z, send, recv):
    b = lax.axis_index("blk")
    x = lax.axis_index("rep")
    c = lax.rem(b, 2)
    y = lax.rem(b // 2, NY)
    z = b // (2 * NY)

    def at_x(d):
        return {"blk": b, "rep": lax.rem(x + d, NX)}

    def at_y(d):
        return {"blk": (z * NY + lax.rem(y + d, NY)) * 2 + c, "rep": x}

    def at_z(d):
        return {"blk": (lax.rem(z + d, NZ) * NY + y) * 2 + c, "rep": x}

    at_c = {"blk": b + 1 - 2 * c, "rep": x}
    partners = [at_x(d) for d in range(1, NX)] + [at_y(d) for d in range(1, NY)]
    partners += [at_z(d) for d in range(1, NZ)] + [at_c]
    barrier = pltpu.get_barrier_semaphore()
    for partner in partners:
        pl.semaphore_signal(barrier, inc=1, device_id=partner, device_id_type=pl.DeviceIdType.MESH)
    pl.semaphore_wait(barrier, len(partners))

    started = []

    def push(source, target, device):
        k = len(started)
        copy = pltpu.make_async_remote_copy(
            src_ref=source,
            dst_ref=target,
            send_sem=send.at[k],
            recv_sem=recv.at[k],
            device_id=device,
            device_id_type=pl.DeviceIdType.MESH,
        )
        copy.start()
        started.append(copy)
        return copy

    quarter = BI // NX

    def piece(n, count):
        return pl.ds(pl.multiple_of(n * count, 8), count)

    tags = [push(code_ref, codes.at[x], at_x(d)) for d in range(1, NX)]
    moves = [
        push(pb_ref.at[:, pl.ds(pl.multiple_of(lax.rem(x + d, NX) * quarter, quarter), quarter), :], rows.at[x], at_x(d))
        for d in range(1, NX)
    ]
    codes[x] = code_ref[...]
    rows[x] = pb_ref[:, pl.ds(pl.multiple_of(x * quarter, quarter), quarter), :]
    for copy in tags:
        copy.wait_recv()
    along = jnp.concatenate([codes[n][0:1, :] for n in range(NX)], axis=1)
    down = jnp.concatenate([codes[n].T[:, 0:1] for n in range(NX)], axis=0)
    same = (down == along).astype(F32).astype(BF16)
    for copy in moves:
        copy.wait_recv()
    held = rows[...].reshape(RR, RR)
    summed = jnp.dot(same, held, preferred_element_type=F32)
    high = summed.astype(BF16)
    low = (summed - high.astype(F32)).astype(BF16)
    at = 0
    for a in range(4):
        left = held[:, 128 * a : 128 * a + 128]
        strip = dot_tn(left, high[:, 128 * a :]) + dot_tn(left, low[:, 128 * a :])
        for n in range(4 - a):
            g[pl.ds(128 * at, 128), :] = strip[:, 128 * n : 128 * n + 128]
            at += 1

    base = c * HALF
    copy = push(g.at[piece(1 - c, HALF)], from_c, at_c)
    copy.wait_recv()
    g[piece(c, HALF), :] += from_c[...]

    copies = [
        push(g.at[pl.ds(pl.multiple_of(base + lax.rem(x + d, NX) * PART_X, 8), PART_X)], from_x.at[d - 1], at_x(d))
        for d in range(1, NX)
    ]
    for copy in copies:
        copy.wait_recv()
    base = base + x * PART_X
    mine = pl.ds(pl.multiple_of(base, 8), PART_X)
    g[mine, :] = g[mine, :] + from_x[0] + from_x[1] + from_x[2]

    copies = [
        push(g.at[pl.ds(pl.multiple_of(base + lax.rem(y + d, NY) * PART_Y, 8), PART_Y)], from_y.at[d - 1], at_y(d))
        for d in range(1, NY)
    ]
    for copy in copies:
        copy.wait_recv()
    base = base + y * PART_Y
    mine = pl.ds(pl.multiple_of(base, 8), PART_Y)
    from_z[z] = g[mine, :] + from_y[0] + from_y[1] + from_y[2]

    copies = [push(from_z.at[z], from_z.at[z], at_z(d)) for d in range(1, NZ)]
    for copy in copies:
        copy.wait_recv()
    total = from_z[0]
    for n in range(1, NZ):
        total = total + from_z[n]
    o[mine, :] = total

    copies = [push(o.at[mine], o.at[mine], at_y(d)) for d in range(1, NY)]
    for copy in copies:
        copy.wait_recv()
    mine = pl.ds(pl.multiple_of(c * HALF + x * PART_X, 8), PART_X)
    copies = [push(o.at[mine], o.at[mine], at_x(d)) for d in range(1, NX)]
    for copy in copies:
        copy.wait_recv()
    copy = push(o.at[piece(c, HALF)], o.at[piece(c, HALF)], at_c)
    copy.wait_recv()

    for n, (p, q) in enumerate(TILES):
        tile = o[pl.ds(128 * n, 128), :]
        gram_ref[pl.ds(128 * p, 128), pl.ds(128 * q, 128)] = tile
        if p != q:
            gram_ref[pl.ds(128 * q, 128), pl.ds(128 * p, 128)] = tile.T
    for copy in started:
        copy.wait_send()


def gram_all(pb, code):
    copies = 2 * 3 + 1 + 3 + 3 + 7 + 3 + 3 + 1
    return pl.pallas_call(
        gram_kernel,
        out_shape=jax.ShapeDtypeStruct((RR, RR), F32),
        in_specs=[pl.BlockSpec(memory_space=pltpu.VMEM)] * 2,
        out_specs=pl.BlockSpec(memory_space=pltpu.VMEM),
        scratch_shapes=[
            pltpu.VMEM((NX, 4, BI // NX, RR), BF16),
            pltpu.VMEM((NX, 8, 128), F32),
            pltpu.VMEM((PACKED, 128), F32),
            pltpu.VMEM((PACKED, 128), F32),
            pltpu.VMEM((HALF, 128), F32),
            pltpu.VMEM((NX - 1, PART_X, 128), F32),
            pltpu.VMEM((NY - 1, PART_Y, 128), F32),
            pltpu.VMEM((NZ, PART_Y, 128), F32),
            pltpu.SemaphoreType.DMA((copies,)),
            pltpu.SemaphoreType.DMA((copies,)),
        ],
        compiler_params=pltpu.CompilerParams(
            collective_id=0, has_side_effects=True, vmem_limit_bytes=40 * 1024 * 1024
        ),
        name="gram_all",
    )(pb, code)


def orthonormal(matrix):
    inner = jnp.dot(matrix.T, matrix, precision=HIGHEST)
    lower_factor = jnp.linalg.cholesky(inner)
    return jax.scipy.linalg.solve_triangular(lower_factor, matrix.T, lower=True).T


def route_rows(global_id, per_owner, groups, capacity):
    owner_of = global_id // per_owner
    local_id = global_id % per_owner
    slot_range = jnp.arange(global_id.shape[0], dtype=jnp.int32)
    earlier = (owner_of[:, None] == owner_of[None, :]) & (slot_range[:, None] > slot_range[None, :])
    rank_in = jnp.sum(earlier.astype(jnp.int32), axis=1)
    chosen = (owner_of[:, None, None] == jnp.arange(groups, dtype=jnp.int32)[None, :, None]) & (
        rank_in[:, None, None] == jnp.arange(capacity, dtype=jnp.int32)[None, None, :]
    )
    request_table = jnp.sum(jnp.where(chosen, local_id[:, None, None], 0), axis=0)
    return (owner_of, rank_in, request_table)


def body(blocks, coords, counts, factor_b, factor_c, start):
    groups = lax.axis_size("blk")
    slots = blocks.shape[0]
    slab_b = factor_b.T.reshape(R2, -1, BJ).transpose(1, 0, 2)
    slab_c = factor_c.T.reshape(R3, -1, 2 * BK).transpose(1, 0, 2)
    owner_b, rank_b, request_b = route_rows(coords[1], slab_b.shape[0], groups, 2)
    owner_c, rank_c, request_c = route_rows(coords[2], 2 * slab_c.shape[0], groups, 2)
    request = jnp.concatenate([request_b, request_c], axis=1)
    asked = lax.all_to_all(request, "blk", split_axis=0, concat_axis=0, tiled=True)
    reply = jnp.concatenate([slab_b[asked[:, :2]], slab_c[asked[:, 2:] // 2]], axis=2)
    fetched = lax.all_to_all(reply, "blk", split_axis=0, concat_axis=0, tiled=True)
    picks = jnp.stack([owner_b, rank_b, owner_c, rank_c, coords[2] % 2, jnp.broadcast_to(counts, (slots,))])
    partial_rows, rounded = contract(blocks, picks, fetched)
    local_block = coords[0] % IB_DEV
    code = (local_block[:, None] * 32 + jnp.arange(32, dtype=jnp.int32)[None, :]).astype(F32)
    code = jnp.broadcast_to(code.reshape(1, 128), (8, 128))
    gram_matrix = gram_all(rounded, code)
    subspace = orthonormal(start)
    for iteration in range(ITERS):
        subspace = orthonormal(jnp.dot(gram_matrix, subspace, precision=HIGHEST))
    small_gram = jnp.dot(subspace.T, jnp.dot(gram_matrix, subspace, precision=HIGHEST), precision=HIGHEST)
    small_gram = 0.5 * (small_gram + small_gram.T)
    lower_factor = jnp.linalg.cholesky(small_gram)
    weights = jax.scipy.linalg.solve_triangular(lower_factor, subspace.T, lower=True)
    mapped = jnp.dot(weights, partial_rows.reshape(slots * BI, RR).T, precision=HIGHEST)
    rep = lax.axis_size("rep")
    sent = jnp.broadcast_to(mapped[None], (rep,) + mapped.shape)
    blocks_all = jnp.broadcast_to(local_block[None, :], (rep, slots))
    got = lax.all_to_all(sent, "rep", split_axis=0, concat_axis=0, tiled=True)
    got_blocks = lax.all_to_all(blocks_all, "rep", split_axis=0, concat_axis=0, tiled=True)
    wanted = lax.axis_index("rep") * (IB_DEV // rep) + jnp.arange(IB_DEV // rep, dtype=jnp.int32)
    place = (got_blocks.reshape(1, -1) == wanted[:, None]).astype(F32)
    terms = got.reshape(rep, R2, slots, BI)
    out = jnp.zeros((R2, IB_DEV // rep, BI), F32)
    for n in range(rep):
        for s in range(slots):
            out = out + terms[n, :, s][:, None, :] * place[:, n * slots + s][None, :, None]
    return out.reshape(R2, -1).T


def solution(mesh):
    return jax.shard_map(
        body,
        mesh=mesh,
        in_specs=(
            P(("blk", "rep"), None, None),
            P(None, ("blk", "rep")),
            P(("blk", "rep")),
            P("blk", None),
            P("blk", None),
            P(),
        ),
        out_specs=P(("blk", "rep"), None),
        check_vma=False,
    )
```

time: 614 us -> 194 us (0.32)
  waiting for transfers between devices: 344 us -> 44.6 us
  blocking collectives: 77.6 us -> 0 us
  Pallas kernels: 0 us -> 53.3 us
  matrix products: 41.5 us -> 10.1 us
  local copies, waits for them, and re-layouts: 38.9 us -> 10.1 us
  other arithmetic: 62.6 us -> 47.2 us
  between operations: 14.5 us -> 1.16 us
  starting transfers between devices: 33.5 us -> 26.8 us
    psum x1 -> x0, waiting for transfers between devices: 250 us -> none  [body(): lax.psum(jnp.dot(unfolded.T, unfolded, precision=lax.Precision.HIGHEST),...]
    reduce_scatter x1 -> x0, waiting for transfers between devices: 77.7 us -> none  [body(): lax.psum_scatter(place_rows(row_share * lax.axis_size('rep'), local_block...]
    psum x1 -> x0, blocking collectives: 77.6 us -> none  [body(): lax.psum(jnp.dot(mapped.T, mapped, precision=lax.Precision.HIGHEST), ('bl...]
    pallas_call x0 -> x2, Pallas kernels: none -> 53.3 us  [the longest x1 41.2 us: gram_all(): pl.pallas_call(gram_kernel, out_shape=jax.ShapeDtypeStruct((RR, RR), F32)...]
    dot_general x15 -> x12, matrix products: 39.1 us -> 8.47 us  [the longest x4 4.28 us: body(): subspace = orthonormal(jnp.dot(gram_matrix, subspace, precision=HIGHEST))]
    all_to_all x4, waiting for transfers between devices: 16.1 us -> 44.6 us  [the longest x1 29.4 us: body(): lax.all_to_all(reply, 'blk', split_axis=0, concat_axis=0, tiled=True)]
    mul x1, other arithmetic: 18.4 us -> 0.01 us  [body(): small_gram = 0.5 * (small_gram + small_gram.T)]
    reshape x5 -> x1, local copies, waits for them, and re-layouts: 14.5 us -> 0.09 us  [body(): terms = got.reshape(rep, R2, slots, BI)]
  transfers between devices with their start and end apart: 6 -> 4, of which waited for: 5 -> 4; matrix products, arithmetic and copies ran while one was open for 11% -> 7% of each run, Pallas kernels for 0% -> 0%
where the time goes in v1:
time: 194 us; the launch traced here: 193 us
  Pallas kernels  53.3 us (27%)
  other arithmetic  47.2 us (24%)
  waiting for transfers between devices  44.6 us (23%)
  starting transfers between devices  26.8 us (14%)
  local copies, waits for them, and re-layouts  10.1 us (5%)
  matrix products  10.1 us (5%)
    pallas_call x1, Pallas kernels, gram_all(): pl.pallas_call(gram_kernel, out_shape=jax.ShapeDtypeStruct((RR, RR), F32)...  41.2 us
    all_to_all x1, waiting for transfers between devices, body(): lax.all_to_all(reply, 'blk', split_axis=0, concat_axis=0, tiled=True)  29.4 us
    another operation x15, other arithmetic, orthonormal(): lower_factor = jnp.linalg.cholesky(inner)  18 us
    another operation x10, other arithmetic, orthonormal(): jax.scipy.linalg.solve_triangular(lower_factor, matrix.T, lower=True)  15.4 us
    all_to_all x1, starting transfers between devices, body(): lax.all_to_all(request, 'blk', split_axis=0, concat_axis=0, tiled=True)  13.2 us
    pallas_call x1, Pallas kernels, contract(): pl.pallas_call(contract_kernel, grid_spec=pltpu.PrefetchScalarGridSpec(nu...  12.1 us
    all_to_all x1, waiting for transfers between devices, body(): lax.all_to_all(request, 'blk', split_axis=0, concat_axis=0, tiled=True)  7.42 us
    all_to_all x1, waiting for transfers between devices, body(): got = lax.all_to_all(sent, 'rep', split_axis=0, concat_axis=0, tiled=True)  6.85 us
  transfers between devices with their start and end apart: 4, of which 4 were waited for; matrix products, arithmetic and copies ran while one was open for 7% of the time, Pallas kernels for 0%

profile of v1, /device:TPU:1, one launch (start us, length us, event | category | flops | bytes accessed | tf_op | source)
XLA Modules:
  0.0 193.2 jit_solution(9357263771343848532)
XLA Ops:
  4.4 13.2 %all-to-all-start = ((s32[64,1,4]{2,1,0:T(1,128)}), s32[64,1,4]{2,1,0:T(1,128)S(1)}, u32[]{:S(2)}, u32[]{:S(2)}) async-start(s32[64,1,4]{2,1,0:T(1,128)} %bitcast.9), calls=%async_computation | async-start | bytes 65536 | tf_op jit(solution)/shard_map/all_to_all | solution.py:273
  17.6 1.1 fusion.65
  19.4 7.4 %all-to-all-done = s32[64,1,4]{2,1,0:T(1,128)S(1)} async-done(((s32[64,1,4]{2,1,0:T(1,128)}), s32[64,1,4]{2,1,0:T(1,128)S(1)}, u32[]{:S(2)}, u32[]{:S(2)}) %all-to-all-start) | async-done | bytes 1056 | tf_op jit(solution)/shard_map/all_to_all | solution.py:273
  27.4 4.0 %all-to-all-start.3 = ((s32[4,1,4]{2,1,0:T(1,128)}), s32[4,1,4]{2,1,0:T(1,128)S(1)}, u32[]{:S(2)}, u32[]{:S(2)}) async-start(s32[4,1,4]{2,1,0:T(1,128)} %broadcast_in_dim.36), calls=%async_computation.3 | async-start | bytes 4096 | tf_op jit(solution)/shard_map/all_to_all | solution.py:294
  33.3 1.3 pad_maximum_fusion
  34.6 0.9 all-to-all-done.3
  35.5 6.2 %all-to-all-start.1 = ((bf16[64,2,48,128]{3,2,1,0:T(8,128)(2,1)}), bf16[64,2,48,128]{3,2,1,0:T(8,128)(2,1)S(1)}, u32[]{:S(2)}, u32[]{:S(2)}) async-start(bf16[64,2,48,128]{3,2,1,0:T(8,128)(2,1)} %pad_maximum_fusion), calls=%async_computation.1 | async-start | bytes 3145728 | tf_op jit(solution)/shard_map/all_to_all | solution.py:275
  42.6 2.9 %cholesky.104 = f32[32,32]{1,0:T(8,128)S(1)} custom-call(f32[32,32]{1,0:T(8,128)S(1)} %fusion.47), custom_call_target="Cholesky" | custom-call | tf_op jit(solution)/shard_map/jit(cholesky)/cholesky | solution.py:248
  46.8 2.4 %custom-call.10 = f32[1,32,32]{1,2,0:T(8,128)S(1)} custom-call(f32[1,32,32]{2,1,0:T(8,128)S(1)} %fusion.28), custom_call_target="InvertDiagBlocksLowerTriangular" | custom-call | tf_op jit(solution)/shard_map/jit(_solve_triangular)/triangular_solve | solution.py:249
  51.5 29.4 %all-to-all-done.1.c_ref.b_ref = bf16[64,2,48,128]{3,2,1,0:T(8,128)(2,1)S(1)} async-done(((bf16[64,2,48,128]{3,2,1,0:T(8,128)(2,1)}), bf16[64,2,48,128]{3,2,1,0:T(8,128)(2,1)S(1)}, u32[]{:S(2)}, u32[]{:S(2)}) %all-to-all-start.1) | async-done | bytes 1572896 | tf_op jit(solution)/shard_map/all_to_all | solution.py:275
  80.8 3.4 %copy-done.1 = bf16[4,128,8192]{2,1,0:T(8,128)(2,1)S(1)} copy-done((bf16[4,128,8192]{2,1,0:T(8,128)(2,1)S(1)}, bf16[4,128,8192]{2,1,0:T(8,128)(2,1)}, u32[]{:S(2)}) %copy-start.1) | copy-done | bytes 8388632
  84.2 12.1 %contract.1 = (f32[4,128,512]{2,1,0:T(8,128)S(1)}, bf16[4,128,512]{2,1,0:T(8,128)(2,1)S(1)}) custom-call(s32[6,4]{1,0:T(8,128)S(1)} %stack.14.pick_ref, bf16[4,128,8192]{2,1,0:T(8,128)(2,1)S(1)} %copy-done.1, bf16[64,2,48,128]{3,2,1,0:T(8,128)(2,1)S(1)} %all-to-all-done.1.c_ref.b_ref, bf16[64,2,48,128]{3,2,1,0:T(8,128)(2,1)S(1)} %all-to-all-done.1.c_ref.b_ref), custom_call_target="tpu_custom_call" | custom-call | tf_op jit(solution)/shard_map/contract/pallas_call | solution.py:73
  96.4 41.2 %gram_all.1 = f32[512,512]{1,0:T(8,128)S(1)} custom-call(bf16[4,128,512]{2,1,0:T(8,128)(2,1)S(1)} %get-tuple-element.9.pb_ref, f32[8,128]{1,0:T(8,128)S(1)} %broadcast_in_dim.33.code_ref), custom_call_target="tpu_custom_call" | custom-call | tf_op jit(solution)/shard_map/gram_all/pallas_call | solution.py:222
  137.5 1.1 fusion.66
  138.9 2.9 %cholesky.115 = f32[32,32]{1,0:T(8,128)S(1)} custom-call(f32[32,32]{1,0:T(8,128)S(1)} %fusion.45), custom_call_target="Cholesky" | custom-call | tf_op jit(solution)/shard_map/jit(cholesky)/cholesky | solution.py:248
  143.2 2.4 %custom-call.11 = f32[1,32,32]{1,2,0:T(8,128)S(1)} custom-call(f32[1,32,32]{2,1,0:T(8,128)S(1)} %fusion.29), custom_call_target="InvertDiagBlocksLowerTriangular" | custom-call | tf_op jit(solution)/shard_map/jit(_solve_triangular)/triangular_solve | solution.py:249
  145.9 1.1 fusion.68
  147.2 2.9 %cholesky.126 = f32[32,32]{1,0:T(8,128)S(1)} custom-call(f32[32,32]{1,0:T(8,128)S(1)} %fusion.43), custom_call_target="Cholesky" | custom-call | tf_op jit(solution)/shard_map/jit(cholesky)/cholesky | solution.py:248
  151.5 2.4 %custom-call.12 = f32[1,32,32]{1,2,0:T(8,128)S(1)} custom-call(f32[1,32,32]{2,1,0:T(8,128)S(1)} %fusion.30), custom_call_target="InvertDiagBlocksLowerTriangular" | custom-call | tf_op jit(solution)/shard_map/jit(_solve_triangular)/triangular_solve | solution.py:249
  154.2 1.1 fusion.70
  155.6 2.9 %cholesky.137 = f32[32,32]{1,0:T(8,128)S(1)} custom-call(f32[32,32]{1,0:T(8,128)S(1)} %fusion.41), custom_call_target="Cholesky" | custom-call | tf_op jit(solution)/shard_map/jit(cholesky)/cholesky | solution.py:248
  159.8 2.4 %custom-call.13 = f32[1,32,32]{1,2,0:T(8,128)S(1)} custom-call(f32[1,32,32]{2,1,0:T(8,128)S(1)} %fusion.31), custom_call_target="InvertDiagBlocksLowerTriangular" | custom-call | tf_op jit(solution)/shard_map/jit(_solve_triangular)/triangular_solve | solution.py:249
  162.6 1.1 fusion.72
  163.9 2.9 %cholesky.148 = f32[32,32]{1,0:T(8,128)S(1)} custom-call(f32[32,32]{1,0:T(8,128)S(1)} %fusion.39), custom_call_target="Cholesky" | custom-call | tf_op jit(solution)/shard_map/jit(cholesky)/cholesky | solution.py:248
  168.2 2.4 %custom-call.14 = f32[1,32,32]{1,2,0:T(8,128)S(1)} custom-call(f32[1,32,32]{2,1,0:T(8,128)S(1)} %fusion.32), custom_call_target="InvertDiagBlocksLowerTriangular" | custom-call | tf_op jit(solution)/shard_map/jit(_solve_triangular)/triangular_solve | solution.py:249
  170.9 1.1 fusion.74
  172.3 2.9 %cholesky.159 = f32[32,32]{1,0:T(8,128)S(1)} custom-call(f32[32,32]{1,0:T(8,128)S(1)} %fusion.36), custom_call_target="Cholesky" | custom-call | tf_op jit(solution)/shard_map/jit(cholesky)/cholesky | solution.py:287
  176.6 2.4 %custom-call.15 = f32[1,32,32]{1,2,0:T(8,128)S(1)} custom-call(f32[1,32,32]{2,1,0:T(8,128)S(1)} %fusion.33), custom_call_target="InvertDiagBlocksLowerTriangular" | custom-call | tf_op jit(solution)/shard_map/jit(_solve_triangular)/triangular_solve | solution.py:288
  179.3 1.0 fusion.76
  181.1 3.4 %all-to-all-start.2 = ((f32[4,32,512]{2,1,0:T(8,128)}), f32[4,32,512]{2,1,0:T(8,128)S(1)}, u32[]{:S(2)}, u32[]{:S(2)}) async-start(f32[4,32,512]{2,1,0:T(8,128)} %broadcast_in_dim.35), calls=%async_computation.2 | async-start | bytes 524288 | tf_op jit(solution)/shard_map/all_to_all | solution.py:293
  184.6 6.9 %all-to-all-done.2 = f32[4,32,512]{2,1,0:T(8,128)S(1)} async-done(((f32[4,32,512]{2,1,0:T(8,128)}), f32[4,32,512]{2,1,0:T(8,128)S(1)}, u32[]{:S(2)}, u32[]{:S(2)}) %all-to-all-start.2) | async-done | bytes 262176 | tf_op jit(solution)/shard_map/all_to_all | solution.py:293
  192.0 1.2 fusion.1
  (109 shorter events, 22.0 us)
Async XLA Ops:
  0.0 17.6 %copy-start = (bf16[2048,32]{0,1:T(8,128)(2,1)S(1)}, bf16[2048,32]{0,1:T(8,128)(2,1)}, u32[]{:S(2)}) copy-start(bf16[2048,32]{0,1:T(8,128)(2,1)} %param.12) | copy-start | bytes 393220
  4.4 22.5 %all-to-all-start = ((s32[64,1,4]{2,1,0:T(1,128)}), s32[64,1,4]{2,1,0:T(1,128)S(1)}, u32[]{:S(2)}, u32[]{:S(2)}) async-start(s32[64,1,4]{2,1,0:T(1,128)} %bitcast.9), calls=%async_computation | async-start | bytes 65536 | tf_op jit(solution)/shard_map/all_to_all | solution.py:273
  27.4 8.0 %all-to-all-start.3 = ((s32[4,1,4]{2,1,0:T(1,128)}), s32[4,1,4]{2,1,0:T(1,128)S(1)}, u32[]{:S(2)}, u32[]{:S(2)}) async-start(s32[4,1,4]{2,1,0:T(1,128)} %broadcast_in_dim.36), calls=%async_computation.3 | async-start | bytes 4096 | tf_op jit(solution)/shard_map/all_to_all | solution.py:294
  34.6 14.8 %copy-start.2 = (f32[512,32]{0,1:T(8,128)S(1)}, f32[512,32]{0,1:T(8,128)}, u32[]{:S(2)}) copy-start(f32[512,32]{0,1:T(8,128)} %param.14) | copy-start | bytes 196612
  35.5 45.3 %all-to-all-start.1 = ((bf16[64,2,48,128]{3,2,1,0:T(8,128)(2,1)}), bf16[64,2,48,128]{3,2,1,0:T(8,128)(2,1)S(1)}, u32[]{:S(2)}, u32[]{:S(2)}) async-start(bf16[64,2,48,128]{3,2,1,0:T(8,128)(2,1)} %pad_maximum_fusion), calls=%async_computation.1 | async-start | bytes 3145728 | tf_op jit(solution)/shard_map/all_to_all | solution.py:275
  80.8 3.4 %copy-start.1 = (bf16[4,128,8192]{2,1,0:T(8,128)(2,1)S(1)}, bf16[4,128,8192]{2,1,0:T(8,128)(2,1)}, u32[]{:S(2)}) copy-start(bf16[4,128,8192]{2,1,0:T(8,128)(2,1)} %x_ref.1) | copy-start | bytes 25165828
  181.1 10.3 %all-to-all-start.2 = ((f32[4,32,512]{2,1,0:T(8,128)}), f32[4,32,512]{2,1,0:T(8,128)S(1)}, u32[]{:S(2)}, u32[]{:S(2)}) async-start(f32[4,32,512]{2,1,0:T(8,128)} %broadcast_in_dim.35), calls=%async_computation.2 | async-start | bytes 524288 | tf_op jit(solution)/shard_map/all_to_all | solution.py:293

commit v2 on v1

--- a/solution.py
+++ b/solution.py
@@ -20,7 +20,6 @@
 HALF = PACKED // 2
 PART_X = HALF // NX
 PART_Y = PART_X // NY
-HIGHEST = lax.Precision.HIGHEST
 F32 = jnp.float32
 BF16 = jnp.bfloat16
 TILES = [(a, b) for a in range(4) for b in range(a, 4)]
@@ -38,7 +37,7 @@
     return lax.broadcasted_iota(jnp.int32, shape, dim)
 
 
-def contract_kernel(pick_ref, x_ref, c_ref, b_ref, p_ref, pb_ref):
+def contract_kernel(pick_ref, x_ref, c_ref, b_ref, high_ref, low_ref):
     slot = pl.program_id(0)
     alive = (slot < pick_ref[5, 0]).astype(F32)
     odd = pick_ref[4, slot] > 0
@@ -64,8 +63,9 @@
         expanded = jnp.dot(mode_b, spread_j, preferred_element_type=F32) * keep
         total += dot_nt(folded, expanded.astype(BF16))
     total = total * alive
-    p_ref[0] = total
-    pb_ref[0] = total.astype(BF16)
+    high = total.astype(BF16)
+    high_ref[0] = high
+    low_ref[0] = (total - high.astype(F32)).astype(BF16)
 
 
 def contract(blocks, picks, fetched):
@@ -86,7 +86,7 @@
             ],
         ),
         out_shape=[
-            jax.ShapeDtypeStruct((slots, BI, RR), F32),
+            jax.ShapeDtypeStruct((slots, BI, RR), BF16),
             jax.ShapeDtypeStruct((slots, BI, RR), BF16),
         ],
         compiler_params=pltpu.CompilerParams(vmem_limit_bytes=40 * 1024 * 1024),
@@ -94,7 +94,54 @@
     )(picks, blocks, fetched, fetched)
 
 
-def gram_kernel(pb_ref, code_ref, gram_ref, rows, codes, g, o, from_c, from_x, from_y, from_z, send, recv):
+def split(value):
+    high = value.astype(BF16)
+    rest = value - high.astype(F32)
+    middle = rest.astype(BF16)
+    low = (rest - middle.astype(F32)).astype(BF16)
+    return high, middle, low
+
+
+def inner_product(left, right):
+    lh, lm, ll = split(left)
+    rh, rm, rl = split(right)
+    return dot_nt(
+        jnp.concatenate([lh, lh, lm, lh, ll, lm], axis=1),
+        jnp.concatenate([rh, rm, rh, rl, rh, rm], axis=1),
+    )
+
+
+def fine_dot(left, high, middle, low):
+    lh, lm, ll = split(left)
+    n = left.shape[0]
+    first = jnp.dot(jnp.concatenate([lh, lm, ll], axis=0), high, preferred_element_type=F32)
+    second = jnp.dot(jnp.concatenate([lh, lm], axis=0), middle, preferred_element_type=F32)
+    third = jnp.dot(lh, low, preferred_element_type=F32)
+    small = first[2 * n :] + second[n:] + third
+    return first[:n] + (first[n : 2 * n] + second[:n] + small)
+
+
+def inverse_lower(inner):
+    n = inner.shape[0]
+    unit = (iota((n, n), 0) == iota((n, n), 1)).astype(F32)
+    work = jnp.concatenate([inner, unit], axis=1)
+    row = iota((n, 1), 0)
+    for k in range(n):
+        scale = lax.rsqrt(work[k : k + 1, k : k + 1])
+        pivot = work[k : k + 1, :] * scale
+        column = jnp.where(row > k, work[:, k : k + 1] * scale, 0.0)
+        work = jnp.where(row == k, pivot, work - column * pivot)
+    return work[:, n:]
+
+
+def orthonormal_t(value):
+    return fine_dot(inverse_lower(inner_product(value, value)), *split(value))
+
+
+def factor_kernel(
+    pb_ref, low_ref, code_ref, start_ref, out_ref,
+    rows, codes, g, o, from_c, from_x, from_y, from_z, gh, gm, gl, space, maps, send, recv,
+):
     b = lax.axis_index("blk")
     x = lax.axis_index("rep")
     c = lax.rem(b, 2)
@@ -146,6 +193,7 @@
     ]
     codes[x] = code_ref[...]
     rows[x] = pb_ref[:, pl.ds(pl.multiple_of(x * quarter, quarter), quarter), :]
+    space[...] = orthonormal_t(start_ref[...])
     for copy in tags:
         copy.wait_recv()
     along = jnp.concatenate([codes[n][0:1, :] for n in range(NX)], axis=1)
@@ -210,19 +258,48 @@
 
     for n, (p, q) in enumerate(TILES):
         tile = o[pl.ds(128 * n, 128), :]
-        gram_ref[pl.ds(128 * p, 128), pl.ds(128 * q, 128)] = tile
+        for ref, part in zip((gh, gm, gl), split(tile)):
+            ref[pl.ds(128 * p, 128), pl.ds(128 * q, 128)] = part
         if p != q:
-            gram_ref[pl.ds(128 * q, 128), pl.ds(128 * p, 128)] = tile.T
+            for ref, part in zip((gh, gm, gl), split(tile.T)):
+                ref[pl.ds(128 * q, 128), pl.ds(128 * p, 128)] = part
+
+    def step(n, carry):
+        space[...] = orthonormal_t(fine_dot(space[...], gh[...], gm[...], gl[...]))
+        return carry
+
+    lax.fori_loop(0, ITERS, step, 0)
+    last = space[...]
+    small = inner_product(last, fine_dot(last, gh[...], gm[...], gl[...]))
+    wide = fine_dot(inverse_lower(small), *split(last))
+    wh, wm, _ = split(wide)
+    high = pb_ref[...].reshape(RR, RR)
+    low = low_ref[...].reshape(RR, RR)
+    both = dot_nt(jnp.concatenate([wh, wm], axis=0), high)
+    maps[x] = both[:R2] + (both[R2:] + dot_nt(wh, low))
+    copies = [push(maps.at[x], maps.at[x], at_x(d)) for d in range(1, NX)]
+    first = (x * (IB_DEV // NX)).astype(F32)
+    for copy in copies:
+        copy.wait_recv()
+    outs = [jnp.zeros((R2, BI), F32) for _ in range(IB_DEV // NX)]
+    for n in range(NX):
+        for s in range(4):
+            label = jnp.broadcast_to(codes[n][0:1, 32 * s : 32 * s + 1], (R2, BI)) * (1.0 / 32.0) - first
+            term = maps[n, :, 128 * s : 128 * s + 128]
+            for k in range(IB_DEV // NX):
+                outs[k] = outs[k] + jnp.where(label == float(k), term, 0.0)
+    for k in range(IB_DEV // NX):
+        out_ref[:, 128 * k : 128 * k + 128] = outs[k]
     for copy in started:
         copy.wait_send()
 
 
-def gram_all(pb, code):
-    copies = 2 * 3 + 1 + 3 + 3 + 7 + 3 + 3 + 1
+def factor(pb, low, code, start_t):
+    copies = 2 * 3 + 1 + 3 + 3 + 7 + 3 + 3 + 1 + 3
     return pl.pallas_call(
-        gram_kernel,
-        out_shape=jax.ShapeDtypeStruct((RR, RR), F32),
-        in_specs=[pl.BlockSpec(memory_space=pltpu.VMEM)] * 2,
+        factor_kernel,
+        out_shape=jax.ShapeDtypeStruct((R2, IB_DEV * BI // NX), F32),
+        in_specs=[pl.BlockSpec(memory_space=pltpu.VMEM)] * 4,
         out_specs=pl.BlockSpec(memory_space=pltpu.VMEM),
         scratch_shapes=[
             pltpu.VMEM((NX, 4, BI // NX, RR), BF16),
@@ -233,20 +310,19 @@
             pltpu.VMEM((NX - 1, PART_X, 128), F32),
             pltpu.VMEM((NY - 1, PART_Y, 128), F32),
             pltpu.VMEM((NZ, PART_Y, 128), F32),
+            pltpu.VMEM((RR, RR), BF16),
+            pltpu.VMEM((RR, RR), BF16),
+            pltpu.VMEM((RR, RR), BF16),
+            pltpu.VMEM((R2, RR), F32),
+            pltpu.VMEM((NX, R2, RR), F32),
             pltpu.SemaphoreType.DMA((copies,)),
             pltpu.SemaphoreType.DMA((copies,)),
         ],
         compiler_params=pltpu.CompilerParams(
             collective_id=0, has_side_effects=True, vmem_limit_bytes=40 * 1024 * 1024
         ),
-        name="gram_all",
-    )(pb, code)
-
-
-def orthonormal(matrix):
-    inner = jnp.dot(matrix.T, matrix, precision=HIGHEST)
-    lower_factor = jnp.linalg.cholesky(inner)
-    return jax.scipy.linalg.solve_triangular(lower_factor, matrix.T, lower=True).T
+        name="factor",
+    )(pb, low, code, start_t)
 
 
 def route_rows(global_id, per_owner, groups, capacity):
@@ -274,32 +350,11 @@
     reply = jnp.concatenate([slab_b[asked[:, :2]], slab_c[asked[:, 2:] // 2]], axis=2)
     fetched = lax.all_to_all(reply, "blk", split_axis=0, concat_axis=0, tiled=True)
     picks = jnp.stack([owner_b, rank_b, owner_c, rank_c, coords[2] % 2, jnp.broadcast_to(counts, (slots,))])
-    partial_rows, rounded = contract(blocks, picks, fetched)
+    high, low = contract(blocks, picks, fetched)
     local_block = coords[0] % IB_DEV
     code = (local_block[:, None] * 32 + jnp.arange(32, dtype=jnp.int32)[None, :]).astype(F32)
     code = jnp.broadcast_to(code.reshape(1, 128), (8, 128))
-    gram_matrix = gram_all(rounded, code)
-    subspace = orthonormal(start)
-    for iteration in range(ITERS):
-        subspace = orthonormal(jnp.dot(gram_matrix, subspace, precision=HIGHEST))
-    small_gram = jnp.dot(subspace.T, jnp.dot(gram_matrix, subspace, precision=HIGHEST), precision=HIGHEST)
-    small_gram = 0.5 * (small_gram + small_gram.T)
-    lower_factor = jnp.linalg.cholesky(small_gram)
-    weights = jax.scipy.linalg.solve_triangular(lower_factor, subspace.T, lower=True)
-    mapped = jnp.dot(weights, partial_rows.reshape(slots * BI, RR).T, precision=HIGHEST)
-    rep = lax.axis_size("rep")
-    sent = jnp.broadcast_to(mapped[None], (rep,) + mapped.shape)
-    blocks_all = jnp.broadcast_to(local_block[None, :], (rep, slots))
-    got = lax.all_to_all(sent, "rep", split_axis=0, concat_axis=0, tiled=True)
-    got_blocks = lax.all_to_all(blocks_all, "rep", split_axis=0, concat_axis=0, tiled=True)
-    wanted = lax.axis_index("rep") * (IB_DEV // rep) + jnp.arange(IB_DEV // rep, dtype=jnp.int32)
-    place = (got_blocks.reshape(1, -1) == wanted[:, None]).astype(F32)
-    terms = got.reshape(rep, R2, slots, BI)
-    out = jnp.zeros((R2, IB_DEV // rep, BI), F32)
-    for n in range(rep):
-        for s in range(slots):
-            out = out + terms[n, :, s][:, None, :] * place[:, n * slots + s][None, :, None]
-    return out.reshape(R2, -1).T
+    return factor(high, low, code, start.T).T
 
 
 def solution(mesh):

time: 194 us -> 155 us (0.80)
  other arithmetic: 47.2 us -> 5.07 us
  Pallas kernels: 53.3 us -> 76.6 us
  matrix products: 10.1 us -> 0 us
  starting transfers between devices: 26.8 us -> 17.9 us
  local copies, waits for them, and re-layouts: 10.1 us -> 7.34 us
  waiting for transfers between devices: 44.6 us -> 46.8 us
    another operation x30 -> x0, other arithmetic: 40.1 us -> none  [the longest x15 18 us: orthonormal(): lower_factor = jnp.linalg.cholesky(inner)]
    pallas_call x1, Pallas kernels: 41.2 us -> 64.6 us  [factor(): pl.pallas_call(factor_kernel, out_shape=jax.ShapeDtypeStruct((R2, IB_DEV...]
    all_to_all x1, waiting for transfers between devices: 29.4 us -> 38.3 us  [body(): lax.all_to_all(reply, 'blk', split_axis=0, concat_axis=0, tiled=True)]
    dot_general x12 -> x0, matrix products: 8.47 us -> none  [the longest x4 4.28 us: body(): subspace = orthonormal(jnp.dot(gram_matrix, subspace, precision=HIGHEST))]
    all_to_all x2 -> x0, waiting for transfers between devices: 7.76 us -> none  [the longest x1 6.85 us: body(): got = lax.all_to_all(sent, 'rep', split_axis=0, concat_axis=0, tiled=True)]
    all_to_all x2 -> x0, starting transfers between devices: 7.42 us -> none  [the longest x1 4.01 us: body(): lax.all_to_all(blocks_all, 'rep', split_axis=0, concat_axis=0, tiled=True)]
    unnamed x6 -> x7, local copies, waits for them, and re-layouts: 3.39 us -> 4.05 us
  transfers between devices with their start and end apart: 4 -> 2, of which waited for: 4 -> 2; matrix products, arithmetic and copies ran while one was open for 7% -> 1% of each run, Pallas kernels for 0% -> 0%
where the time goes in v2:
time: 155 us
  Pallas kernels  76.6 us (49%)
  waiting for transfers between devices  46.8 us (30%)
  starting transfers between devices  17.9 us (12%)
  local copies, waits for them, and re-layouts  7.34 us (5%)
  other arithmetic  5.07 us (3%)
    pallas_call x1, Pallas kernels, factor(): pl.pallas_call(factor_kernel, out_shape=jax.ShapeDtypeStruct((R2, IB_DEV...  64.6 us
    all_to_all x1, waiting for transfers between devices, body(): lax.all_to_all(reply, 'blk', split_axis=0, concat_axis=0, tiled=True)  38.3 us
    all_to_all x1, starting transfers between devices, body(): lax.all_to_all(request, 'blk', split_axis=0, concat_axis=0, tiled=True)  13.2 us
    pallas_call x1, Pallas kernels, contract(): pl.pallas_call(contract_kernel, grid_spec=pltpu.PrefetchScalarGridSpec(nu...  12 us
    all_to_all x1, waiting for transfers between devices, body(): lax.all_to_all(request, 'blk', split_axis=0, concat_axis=0, tiled=True)  8.54 us
    all_to_all x1, starting transfers between devices, body(): lax.all_to_all(reply, 'blk', split_axis=0, concat_axis=0, tiled=True)  4.79 us
    unnamed x7, local copies, waits for them, and re-layouts  4.05 us
  transfers between devices with their start and end apart: 2, of which 2 were waited for; matrix products, arithmetic and copies ran while one was open for 1% of the time, Pallas kernels for 0%

profile of v2, /device:TPU:1, one launch (start us, length us, event | category | flops | bytes accessed | tf_op | source)
XLA Modules:
  0.0 154.5 jit_solution(13107256788025815797)
XLA Ops:
  0.0 0.0 copy-start
  0.0 0.8 and_select_fusion.1
  0.8 0.8 and_select_fusion.3
  1.5 0.8 and_select_fusion.2
  2.3 0.7 and_select_fusion.6
  3.0 0.1 iota_compare_fusion.1
  3.1 0.2 convert_reduce_fusion.1
  3.3 0.1 iota_compare_fusion
  3.3 0.2 convert_reduce_fusion
  3.5 0.1 select_reduce_fusion
  3.7 0.7 copy.13
  4.4 13.2 %all-to-all-start = ((s32[64,1,4]{2,1,0:T(1,128)}), s32[64,1,4]{2,1,0:T(1,128)S(1)}, u32[]{:S(2)}, u32[]{:S(2)}) async-start(s32[64,1,4]{2,1,0:T(1,128)} %bitcast.9), calls=%async_computation | async-start | bytes 65536 | tf_op jit(solution)/shard_map/all_to_all | solution.py:349
  17.5 0.0 copy-done
  17.6 0.7 bitcast_bitcast_fusion.1
  18.3 8.5 %all-to-all-done = s32[64,1,4]{2,1,0:T(1,128)S(1)} async-done(((s32[64,1,4]{2,1,0:T(1,128)}), s32[64,1,4]{2,1,0:T(1,128)S(1)}, u32[]{:S(2)}, u32[]{:S(2)}) %all-to-all-start) | async-done | bytes 1056 | tf_op jit(solution)/shard_map/all_to_all | solution.py:349
  26.8 0.1 compare_select_fusion.1
  26.9 0.1 reshape.299
  27.1 0.1 reshape.307
  27.2 0.8 gather_fusion
  28.0 0.7 gather_fusion.1
  28.7 1.3 pad_maximum_fusion
  30.0 4.8 %all-to-all-start.1 = ((bf16[64,2,48,128]{3,2,1,0:T(8,128)(2,1)}), bf16[64,2,48,128]{3,2,1,0:T(8,128)(2,1)S(1)}, u32[]{:S(2)}, u32[]{:S(2)}) async-start(bf16[64,2,48,128]{3,2,1,0:T(8,128)(2,1)} %pad_maximum_fusion), calls=%async_computation.1 | async-start | bytes 3145728 | tf_op jit(solution)/shard_map/all_to_all | solution.py:351
  35.4 0.1 add_convert_fusion
  35.5 0.1 convert_element_type.19
  35.6 38.3 %all-to-all-done.1.c_ref.b_ref = bf16[64,2,48,128]{3,2,1,0:T(8,128)(2,1)S(1)} async-done(((bf16[64,2,48,128]{3,2,1,0:T(8,128)(2,1)}), bf16[64,2,48,128]{3,2,1,0:T(8,128)(2,1)S(1)}, u32[]{:S(2)}, u32[]{:S(2)}) %all-to-all-start.1) | async-done | bytes 1572896 | tf_op jit(solution)/shard_map/all_to_all | solution.py:351
  73.9 0.0 copy-start.1
  73.9 3.4 %copy-done.1 = bf16[4,128,8192]{2,1,0:T(8,128)(2,1)S(1)} copy-done((bf16[4,128,8192]{2,1,0:T(8,128)(2,1)S(1)}, bf16[4,128,8192]{2,1,0:T(8,128)(2,1)}, u32[]{:S(2)}) %copy-start.1) | copy-done | bytes 8388632
  77.3 0.0 copy-start.2
  77.3 12.0 %contract.1 = (bf16[4,128,512]{2,1,0:T(8,128)(2,1)S(1)}, bf16[4,128,512]{2,1,0:T(8,128)(2,1)S(1)}) custom-call(s32[6,4]{1,0:T(8,128)S(1)} %stack.14.pick_ref, bf16[4,128,8192]{2,1,0:T(8,128)(2,1)S(1)} %copy-done.1, bf16[64,2,48,128]{3,2,1,0:T(8,128)(2,1)S(1)} %all-to-all-done.1.c_ref.b_ref, bf16[64,2,48,128]{3,2,1,0:T(8,128)(2,1)S(1)} %all-to-all-done.1.c_ref.b_ref), custom_call_target="tpu_custom_call" | custom-call | tf_op jit(solution)/shard_map/contract/pallas_call | solution.py:73
  89.2 0.0 copy-done.2
  89.2 64.6 %factor.1 = f32[32,1024]{1,0:T(8,128)S(1)} custom-call(bf16[4,128,512]{2,1,0:T(8,128)(2,1)S(1)} %get-tuple-element.7.pb_ref, bf16[4,128,512]{2,1,0:T(8,128)(2,1)S(1)} %get-tuple-element.8.low_ref, f32[8,128]{1,0:T(8,128)S(1)} %broadcast_in_dim.29.code_ref, f32[32,512]{1,0:T(8,128)S(1)} %bitcast.55), custom_call_target="tpu_custom_call" | custom-call | tf_op jit(solution)/shard_map/factor/pallas_call | solution.py:299
  153.9 0.7 copy.21
  (9 shorter events, 0.1 us)
Async XLA Ops:
  0.0 17.5 %copy-start = (bf16[2048,32]{0,1:T(8,128)(2,1)S(1)}, bf16[2048,32]{0,1:T(8,128)(2,1)}, u32[]{:S(2)}) copy-start(bf16[2048,32]{0,1:T(8,128)(2,1)} %param.9) | copy-start | bytes 393220
  4.4 22.5 %all-to-all-start = ((s32[64,1,4]{2,1,0:T(1,128)}), s32[64,1,4]{2,1,0:T(1,128)S(1)}, u32[]{:S(2)}, u32[]{:S(2)}) async-start(s32[64,1,4]{2,1,0:T(1,128)} %bitcast.9), calls=%async_computation | async-start | bytes 65536 | tf_op jit(solution)/shard_map/all_to_all | solution.py:349
  30.0 43.9 %all-to-all-start.1 = ((bf16[64,2,48,128]{3,2,1,0:T(8,128)(2,1)}), bf16[64,2,48,128]{3,2,1,0:T(8,128)(2,1)S(1)}, u32[]{:S(2)}, u32[]{:S(2)}) async-start(bf16[64,2,48,128]{3,2,1,0:T(8,128)(2,1)} %pad_maximum_fusion), calls=%async_computation.1 | async-start | bytes 3145728 | tf_op jit(solution)/shard_map/all_to_all | solution.py:351
  73.9 3.4 %copy-start.1 = (bf16[4,128,8192]{2,1,0:T(8,128)(2,1)S(1)}, bf16[4,128,8192]{2,1,0:T(8,128)(2,1)}, u32[]{:S(2)}) copy-start(bf16[4,128,8192]{2,1,0:T(8,128)(2,1)} %x_ref.1) | copy-start | bytes 25165828
  77.3 12.0 %copy-start.2 = (f32[512,32]{0,1:T(8,128)S(1)}, f32[512,32]{0,1:T(8,128)}, u32[]{:S(2)}) copy-start(f32[512,32]{0,1:T(8,128)} %param.11) | copy-start | bytes 196612

commit v3 on v2

--- a/solution.py
+++ b/solution.py
@@ -12,6 +12,7 @@
 R3 = 16
 RR = 512
 IB_DEV = 32
+NB = 4
 ITERS = 4
 NX = 4
 NY = 4
@@ -37,61 +38,28 @@
     return lax.broadcasted_iota(jnp.int32, shape, dim)
 
 
-def contract_kernel(pick_ref, x_ref, c_ref, b_ref, high_ref, low_ref):
-    slot = pl.program_id(0)
-    alive = (slot < pick_ref[5, 0]).astype(F32)
-    odd = pick_ref[4, slot] > 0
-    pair = c_ref[0, 0].astype(F32)
-    mode_c = jnp.where(odd, pair[:, BK:], pair[:, :BK])
+def fold_slot(held_x, slot, pair, odd, folded):
+    pair = pair.astype(F32)
+    mode_c = pair[:, :BK] * (1.0 - odd) + pair[:, BK:] * odd
     wide = jnp.concatenate([mode_c] * 8, axis=1)
     tall = jnp.concatenate([wide] * 8, axis=0)
     fold_mask = iota((128, 512), 0) // R3 == iota((128, 512), 1) // BK
     fold_t = jnp.where(fold_mask, tall, 0.0).astype(BF16)
+    for t in range(16):
+        part = dot_nt(held_x[slot, :, 512 * t : 512 * t + 512], fold_t)
+        folded[slot, :, 128 * t : 128 * t + 128] = part.astype(BF16)
+
+
+def contract_slot(folded, slot, block_b, alive):
     spread_q = (iota((RR, R2), 0) // R3 == iota((RR, R2), 1)).astype(F32).astype(BF16)
-    mode_b = jnp.dot(spread_q, b_ref[0, 0], preferred_element_type=F32).astype(BF16)
+    mode_b = jnp.dot(spread_q, block_b, preferred_element_type=F32).astype(BF16)
     keep = (iota((RR, 256), 0) % R3 == iota((RR, 256), 1) % R3).astype(F32)
     total = jnp.zeros((BI, RR), F32)
     for t in range(8):
-        folded = jnp.concatenate(
-            [
-                dot_nt(x_ref[0, :, pl.ds((2 * t + h) * 512, 512)], fold_t).astype(BF16)
-                for h in range(2)
-            ],
-            axis=1,
-        )
         spread_j = (iota((BJ, 256), 0) == 16 * t + iota((BJ, 256), 1) // R3).astype(F32).astype(BF16)
         expanded = jnp.dot(mode_b, spread_j, preferred_element_type=F32) * keep
-        total += dot_nt(folded, expanded.astype(BF16))
-    total = total * alive
-    high = total.astype(BF16)
-    high_ref[0] = high
-    low_ref[0] = (total - high.astype(F32)).astype(BF16)
-
-
-def contract(blocks, picks, fetched):
-    slots = blocks.shape[0]
-    return pl.pallas_call(
-        contract_kernel,
-        grid_spec=pltpu.PrefetchScalarGridSpec(
-            num_scalar_prefetch=1,
-            grid=(slots,),
-            in_specs=[
-                pl.BlockSpec((1, BI, BJ * BK), lambda s, pick: (s, 0, 0)),
-                pl.BlockSpec((1, 1, R3, 128), lambda s, pick: (pick[2, s], pick[3, s], 2, 0)),
-                pl.BlockSpec((1, 1, R2, 128), lambda s, pick: (pick[0, s], pick[1, s], 0, 0)),
-            ],
-            out_specs=[
-                pl.BlockSpec((1, BI, RR), lambda s, pick: (s, 0, 0)),
-                pl.BlockSpec((1, BI, RR), lambda s, pick: (s, 0, 0)),
-            ],
-        ),
-        out_shape=[
-            jax.ShapeDtypeStruct((slots, BI, RR), BF16),
-            jax.ShapeDtypeStruct((slots, BI, RR), BF16),
-        ],
-        compiler_params=pltpu.CompilerParams(vmem_limit_bytes=40 * 1024 * 1024),
-        name="contract",
-    )(picks, blocks, fetched, fetched)
+        total += dot_nt(folded[slot, :, 256 * t : 256 * t + 256], expanded.astype(BF16))
+    return total * alive
 
 
 def split(value):
@@ -139,8 +107,9 @@
 
 
 def factor_kernel(
-    pb_ref, low_ref, code_ref, start_ref, out_ref,
-    rows, codes, g, o, from_c, from_x, from_y, from_z, gh, gm, gl, space, maps, send, recv,
+    blocks_ref, coords_ref, counts_ref, info_ref, fb_ref, fc_ref, start_ref, out_ref,
+    held_x, plane_b, plane_c, infos, asked, give_b, give_c, got_b, got_c, folded, high_ref, low_ref,
+    rows, codes, g, o, from_c, from_x, from_y, from_z, gh, gm, gl, space, maps, send, recv, load,
 ):
     b = lax.axis_index("blk")
     x = lax.axis_index("rep")
@@ -160,6 +129,9 @@
     at_c = {"blk": b + 1 - 2 * c, "rep": x}
     partners = [at_x(d) for d in range(1, NX)] + [at_y(d) for d in range(1, NY)]
     partners += [at_z(d) for d in range(1, NZ)] + [at_c]
+    loads = [pltpu.make_async_copy(blocks_ref.at[s], held_x.at[s], load.at[s]) for s in range(NB)]
+    for copy in loads:
+        copy.start()
     barrier = pltpu.get_barrier_semaphore()
     for partner in partners:
         pl.semaphore_signal(barrier, inc=1, device_id=partner, device_id_type=pl.DeviceIdType.MESH)
@@ -186,18 +158,92 @@
     def piece(n, count):
         return pl.ds(pl.multiple_of(n * count, 8), count)
 
-    tags = [push(code_ref, codes.at[x], at_x(d)) for d in range(1, NX)]
+    wishes = [push(info_ref, infos.at[z], at_z(d)) for d in range(1, NZ)]
+    tags = [push(info_ref, codes.at[x], at_x(d)) for d in range(1, NX)]
+    infos[z] = info_ref[...]
+    codes[x] = info_ref[...]
+
+    own = y * 2 + c
+    planes = ((plane_c, 4), (plane_b, 16))
+
+    def part(n, place):
+        plane, count = planes[n]
+        return plane.at[pl.ds(pl.multiple_of(place * count, count), count)]
+
+    for n, ref in ((0, fc_ref), (1, fb_ref)):
+        plane, count = planes[n]
+        for k in range(count):
+            plane[own * count + k] = ref[:, 128 * k : 128 * k + 128]
+    along_y = [[push(part(n, own), part(n, own), at_y(d)) for d in range(1, NY)] for n in range(2)]
+    across = [[push(part(n, own), part(n, own), at_c)] for n in range(2)]
+    space[...] = orthonormal_t(start_ref[...])
+    for copy in wishes:
+        copy.wait_recv()
+    copy = pltpu.make_async_copy(infos, asked, load.at[NB])
+    copy.start()
+    copy.wait()
+
+    def relay(n):
+        for d in range(1, NY):
+            along_y[n][d - 1].wait_recv()
+            place = lax.rem(y + NY - d, NY) * 2 + c
+            across[n].append(push(part(n, place), part(n, place), at_c))
+        for copy in across[n]:
+            copy.wait_recv()
+
+    relay(0)
+    def answer(plane, mode, shift, mask, give, got):
+        sent = []
+        for d in range(NZ):
+            t = lax.rem(z + d, NZ)
+            for s in range(NB):
+                block = plane[(asked[t, 1, NB * mode + s] >> shift) & mask]
+                if d == 0:
+                    got[z * NB + s] = block
+                else:
+                    give[d - 1, s] = block
+            if d > 0:
+                target = got.at[pl.ds(pl.multiple_of(z * NB, NB), NB)]
+                sent.append(push(give.at[d - 1], target, at_z(d)))
+        return sent
+
+    sent_c = answer(plane_c, 1, 1, 31, give_c, got_c)
+    relay(1)
+    sent_b = answer(plane_b, 0, 0, 127, give_b, got_b)
+    for copy in loads:
+        copy.wait()
+    for copy in sent_c:
+        copy.wait_recv()
+
+    def fold_step(s, carry):
+        wish = coords_ref[2, s]
+        fold_slot(held_x, s, got_c[(wish >> 6) * NB + s], (wish & 1).astype(F32), folded)
+        return carry
+
+    lax.fori_loop(0, NB, fold_step, 0)
+    for copy in sent_b:
+        copy.wait_recv()
+
+    def contract_step(s, carry):
+        alive = jnp.clip(counts_ref[0] - s, 0, 1).astype(F32)
+        total = contract_slot(folded, s, got_b[(coords_ref[1, s] >> 7) * NB + s], alive)
+        high = total.astype(BF16)
+        high_ref[s] = high
+        low_ref[s] = (total - high.astype(F32)).astype(BF16)
+        return carry
+
+    lax.fori_loop(0, NB, contract_step, 0)
+
     moves = [
-        push(pb_ref.at[:, pl.ds(pl.multiple_of(lax.rem(x + d, NX) * quarter, quarter), quarter), :], rows.at[x], at_x(d))
+        push(high_ref.at[:, pl.ds(pl.multiple_of(lax.rem(x + d, NX) * quarter, quarter), quarter), :], rows.at[x], at_x(d))
         for d in range(1, NX)
     ]
-    codes[x] = code_ref[...]
-    rows[x] = pb_ref[:, pl.ds(pl.multiple_of(x * quarter, quarter), quarter), :]
-    space[...] = orthonormal_t(start_ref[...])
+    rows[x] = high_ref[:, pl.ds(pl.multiple_of(x * quarter, quarter), quarter), :]
     for copy in tags:
         copy.wait_recv()
-    along = jnp.concatenate([codes[n][0:1, :] for n in range(NX)], axis=1)
-    down = jnp.concatenate([codes[n].T[:, 0:1] for n in range(NX)], axis=0)
+    labels = [codes[n].astype(F32) for n in range(NX)]
+    along = jnp.concatenate([label[0:1, :] for label in labels], axis=1)
+    down = jnp.concatenate([label.T[:, 0:1] for label in labels], axis=0)
     same = (down == along).astype(F32).astype(BF16)
     for copy in moves:
         copy.wait_recv()
@@ -273,7 +319,7 @@
     small = inner_product(last, fine_dot(last, gh[...], gm[...], gl[...]))
     wide = fine_dot(inverse_lower(small), *split(last))
     wh, wm, _ = split(wide)
-    high = pb_ref[...].reshape(RR, RR)
+    high = high_ref[...].reshape(RR, RR)
     low = low_ref[...].reshape(RR, RR)
     both = dot_nt(jnp.concatenate([wh, wm], axis=0), high)
     maps[x] = both[:R2] + (both[R2:] + dot_nt(wh, low))
@@ -283,8 +329,8 @@
         copy.wait_recv()
     outs = [jnp.zeros((R2, BI), F32) for _ in range(IB_DEV // NX)]
     for n in range(NX):
-        for s in range(4):
-            label = jnp.broadcast_to(codes[n][0:1, 32 * s : 32 * s + 1], (R2, BI)) * (1.0 / 32.0) - first
+        for s in range(NB):
+            label = jnp.broadcast_to(labels[n][0:1, 32 * s : 32 * s + 1], (R2, BI)) * (1.0 / 32.0) - first
             term = maps[n, :, 128 * s : 128 * s + 128]
             for k in range(IB_DEV // NX):
                 outs[k] = outs[k] + jnp.where(label == float(k), term, 0.0)
@@ -294,16 +340,31 @@
         copy.wait_send()
 
 
-def factor(pb, low, code, start_t):
-    copies = 2 * 3 + 1 + 3 + 3 + 7 + 3 + 3 + 1 + 3
+def factor(blocks, coords, counts, info, slab_b, slab_c, start_t):
+    copies = 65
+    vmem = pl.BlockSpec(memory_space=pltpu.VMEM)
+    smem = pl.BlockSpec(memory_space=pltpu.SMEM)
+    hbm = pl.BlockSpec(memory_space=pltpu.HBM)
     return pl.pallas_call(
         factor_kernel,
         out_shape=jax.ShapeDtypeStruct((R2, IB_DEV * BI // NX), F32),
-        in_specs=[pl.BlockSpec(memory_space=pltpu.VMEM)] * 4,
-        out_specs=pl.BlockSpec(memory_space=pltpu.VMEM),
+        in_specs=[hbm, smem, smem, vmem, vmem, vmem, vmem],
+        out_specs=vmem,
         scratch_shapes=[
-            pltpu.VMEM((NX, 4, BI // NX, RR), BF16),
-            pltpu.VMEM((NX, 8, 128), F32),
+            pltpu.VMEM((NB, BI, BJ * BK), BF16),
+            pltpu.VMEM((2 * NY * 16, R2, BJ), BF16),
+            pltpu.VMEM((2 * NY * 4, R3, 2 * BK), BF16),
+            pltpu.VMEM((NZ, 8, 128), jnp.int32),
+            pltpu.SMEM((NZ, 8, 128), jnp.int32),
+            pltpu.VMEM((NZ - 1, NB, R2, BJ), BF16),
+            pltpu.VMEM((NZ - 1, NB, R3, 2 * BK), BF16),
+            pltpu.VMEM((NZ * NB, R2, BJ), BF16),
+            pltpu.VMEM((NZ * NB, R3, 2 * BK), BF16),
+            pltpu.VMEM((NB, BI, BJ * R3), BF16),
+            pltpu.VMEM((NB, BI, RR), BF16),
+            pltpu.VMEM((NB, BI, RR), BF16),
+            pltpu.VMEM((NX, NB, BI // NX, RR), BF16),
+            pltpu.VMEM((NX, 8, 128), jnp.int32),
             pltpu.VMEM((PACKED, 128), F32),
             pltpu.VMEM((PACKED, 128), F32),
             pltpu.VMEM((HALF, 128), F32),
@@ -317,44 +378,20 @@
             pltpu.VMEM((NX, R2, RR), F32),
             pltpu.SemaphoreType.DMA((copies,)),
             pltpu.SemaphoreType.DMA((copies,)),
+            pltpu.SemaphoreType.DMA((NB + 1,)),
         ],
         compiler_params=pltpu.CompilerParams(
-            collective_id=0, has_side_effects=True, vmem_limit_bytes=40 * 1024 * 1024
+            collective_id=0, has_side_effects=True, vmem_limit_bytes=48 * 1024 * 1024
         ),
         name="factor",
-    )(pb, low, code, start_t)
-
-
-def route_rows(global_id, per_owner, groups, capacity):
-    owner_of = global_id // per_owner
-    local_id = global_id % per_owner
-    slot_range = jnp.arange(global_id.shape[0], dtype=jnp.int32)
-    earlier = (owner_of[:, None] == owner_of[None, :]) & (slot_range[:, None] > slot_range[None, :])
-    rank_in = jnp.sum(earlier.astype(jnp.int32), axis=1)
-    chosen = (owner_of[:, None, None] == jnp.arange(groups, dtype=jnp.int32)[None, :, None]) & (
-        rank_in[:, None, None] == jnp.arange(capacity, dtype=jnp.int32)[None, None, :]
-    )
-    request_table = jnp.sum(jnp.where(chosen, local_id[:, None, None], 0), axis=0)
-    return (owner_of, rank_in, request_table)
+    )(blocks, coords, counts, info, slab_b, slab_c, start_t)
 
 
 def body(blocks, coords, counts, factor_b, factor_c, start):
-    groups = lax.axis_size("blk")
-    slots = blocks.shape[0]
-    slab_b = factor_b.T.reshape(R2, -1, BJ).transpose(1, 0, 2)
-    slab_c = factor_c.T.reshape(R3, -1, 2 * BK).transpose(1, 0, 2)
-    owner_b, rank_b, request_b = route_rows(coords[1], slab_b.shape[0], groups, 2)
-    owner_c, rank_c, request_c = route_rows(coords[2], 2 * slab_c.shape[0], groups, 2)
-    request = jnp.concatenate([request_b, request_c], axis=1)
-    asked = lax.all_to_all(request, "blk", split_axis=0, concat_axis=0, tiled=True)
-    reply = jnp.concatenate([slab_b[asked[:, :2]], slab_c[asked[:, 2:] // 2]], axis=2)
-    fetched = lax.all_to_all(reply, "blk", split_axis=0, concat_axis=0, tiled=True)
-    picks = jnp.stack([owner_b, rank_b, owner_c, rank_c, coords[2] % 2, jnp.broadcast_to(counts, (slots,))])
-    high, low = contract(blocks, picks, fetched)
-    local_block = coords[0] % IB_DEV
-    code = (local_block[:, None] * 32 + jnp.arange(32, dtype=jnp.int32)[None, :]).astype(F32)
-    code = jnp.broadcast_to(code.reshape(1, 128), (8, 128))
-    return factor(high, low, code, start.T).T
+    code = ((coords[0] % IB_DEV)[:, None] * 32 + jnp.arange(32, dtype=jnp.int32)[None, :]).reshape(1, 128)
+    asks = jnp.pad(coords[1:].reshape(1, 2 * NB), ((0, 6), (0, 128 - 2 * NB)))
+    info = jnp.concatenate([code, asks], axis=0)
+    return factor(blocks, coords, counts, info, factor_b.T, factor_c.T, start.T).T
 
 
 def solution(mesh):

time: 155 us -> 106 us (0.68)
  waiting for transfers between devices: 46.8 us -> 0 us
  Pallas kernels: 76.6 us -> 99.4 us
  starting transfers between devices: 17.9 us -> 0 us
  other arithmetic: 5.07 us -> 0.77 us
  local copies, waits for them, and re-layouts: 7.34 us -> 4.65 us
    all_to_all x2 -> x0, waiting for transfers between devices: 46.8 us -> none  [the longest x1 38.3 us: body(): lax.all_to_all(reply, 'blk', split_axis=0, concat_axis=0, tiled=True)]
    pallas_call x1, Pallas kernels: 64.6 us -> 99.4 us  [factor(): pl.pallas_call(factor_kernel, out_shape=jax.ShapeDtypeStruct((R2, IB_DEV...]
    all_to_all x2 -> x0, starting transfers between devices: 17.9 us -> none  [the longest x1 13.2 us: body(): lax.all_to_all(request, 'blk', split_axis=0, concat_axis=0, tiled=True)]
    pallas_call x1 -> x0, Pallas kernels: 12 us -> none  [contract(): pl.pallas_call(contract_kernel, grid_spec=pltpu.PrefetchScalarGridSpec(nu...]
    select_n x5 -> x0, other arithmetic: 3.09 us -> none  [the longest x2 1.54 us: route_rows(): local_id = global_id % per_owner]
    unnamed x7 -> x9, local copies, waits for them, and re-layouts: 4.05 us -> 3.8 us
  transfers between devices with their start and end apart: 2 -> 0, of which waited for: 2 -> 0; matrix products, arithmetic and copies ran while one was open for 1% -> 0% of each run, Pallas kernels for 0% -> 0%
where the time goes in v3:
time: 106 us; the launch traced here: 105 us
  Pallas kernels  99.4 us (94%)
  local copies, waits for them, and re-layouts  4.65 us (4%)
    pallas_call x1, Pallas kernels, factor(): pl.pallas_call(factor_kernel, out_shape=jax.ShapeDtypeStruct((R2, IB_DEV...  99.4 us
    unnamed x9, local copies, waits for them, and re-layouts  3.8 us

profile of v3, /device:TPU:1, one launch (start us, length us, event | category | flops | bytes accessed | tf_op | source)
XLA Modules:
  0.0 105.5 jit_solution(674222194312491511)
XLA Ops:
  0.7 0.7 fusion
  1.3 0.7 slice.7
  2.0 0.1 reshape.49
  2.1 0.1 iota_add_fusion
  2.2 0.1 add.39
  2.3 0.0 copy-start
  2.3 0.9 copy-done
  3.2 0.0 copy-start.1
  3.2 0.8 copy-done.1
  4.0 0.0 copy-start.2
  4.0 0.7 copy-done.2
  4.7 0.0 copy-start.3
  4.7 0.7 copy-done.3
  5.4 99.4 %factor.1 = f32[32,1024]{1,0:T(8,128)S(1)} custom-call(bf16[4,128,8192]{2,1,0:T(8,128)(2,1)} %blocks_ref.1, s32[3,4]{1,0:T(4,128)S(1)} %copy-done.3, s32[1]{0:T(128)S(6)} %copy.8.counts_ref, s32[8,128]{1,0:T(8,128)S(1)} %pad_add_fusion.info_ref, bf16[32,2048]{1,0:T(8,128)(2,1)S(1)} %bitcast.7, bf16[16,512]{1,0:T(8,128)(2,1)S(1)} %bitcast.9, ...), custom_call_target="tpu_custom_call" | custom-call | tf_op jit(solution)/shard_map/factor/pallas_call | solution.py:348
  104.8 0.7 copy.9
  (1 shorter events, 0.0 us)
Async XLA Ops:
  2.3 0.9 copy-start
  3.2 0.8 copy-start.1
  4.0 0.7 copy-start.2
  4.7 0.7 copy-start.3

commit v4 on v3

--- a/solution.py
+++ b/solution.py
@@ -19,8 +19,8 @@
 NZ = 8
 PACKED = 1280
 HALF = PACKED // 2
-PART_X = HALF // NX
-PART_Y = PART_X // NY
+PART_0 = 384
+PART_1 = HALF - PART_0
 F32 = jnp.float32
 BF16 = jnp.bfloat16
 TILES = [(a, b) for a in range(4) for b in range(a, 4)]
@@ -93,13 +93,17 @@
     n = inner.shape[0]
     unit = (iota((n, n), 0) == iota((n, n), 1)).astype(F32)
     work = jnp.concatenate([inner, unit], axis=1)
-    row = iota((n, 1), 0)
-    for k in range(n):
-        scale = lax.rsqrt(work[k : k + 1, k : k + 1])
-        pivot = work[k : k + 1, :] * scale
-        column = jnp.where(row > k, work[:, k : k + 1] * scale, 0.0)
-        work = jnp.where(row == k, pivot, work - column * pivot)
-    return work[:, n:]
+    row = iota((n, 2 * n), 0)
+    for k in range(0, n, 4):
+        columns = [jnp.broadcast_to(work[:, k + t : k + t + 1], (n, 2 * n)) for t in range(4)]
+        for t in range(4):
+            at = k + t
+            inverse = 1.0 / columns[t][at : at + 1]
+            for u in range(t + 1, 4):
+                columns[u] = columns[u] - columns[t] * (columns[u][at : at + 1] * inverse)
+            work = work - jnp.where(row > at, columns[t], 0.0) * (work[at : at + 1] * inverse)
+    diagonal = jnp.sum(work[:, :n] * unit, axis=1, keepdims=True)
+    return work[:, n:] * lax.rsqrt(diagonal)
 
 
 def orthonormal_t(value):
@@ -107,9 +111,10 @@
 
 
 def factor_kernel(
-    blocks_ref, coords_ref, counts_ref, info_ref, fb_ref, fc_ref, start_ref, out_ref,
+    blocks_ref, coords_hbm, counts_hbm, fb_hbm, fc_hbm, start_hbm, out_ref,
+    coords_ref, counts_ref, info_ref, fb_ref, fc_ref, start_ref,
     held_x, plane_b, plane_c, infos, asked, give_b, give_c, got_b, got_c, folded, high_ref, low_ref,
-    rows, codes, g, o, from_c, from_x, from_y, from_z, gh, gm, gl, space, maps, send, recv, load,
+    rows, codes, g, o, from_c, from_u0, from_u1, from_v0, from_v1, from_z, gh, gm, gl, space, maps, far, send, recv, load, feed,
 ):
     b = lax.axis_index("blk")
     x = lax.axis_index("rep")
@@ -130,7 +135,11 @@
     partners = [at_x(d) for d in range(1, NX)] + [at_y(d) for d in range(1, NY)]
     partners += [at_z(d) for d in range(1, NZ)] + [at_c]
     loads = [pltpu.make_async_copy(blocks_ref.at[s], held_x.at[s], load.at[s]) for s in range(NB)]
-    for copy in loads:
+    inputs = (
+        (coords_hbm, coords_ref), (counts_hbm, counts_ref), (fc_hbm, fc_ref), (fb_hbm, fb_ref), (start_hbm, start_ref),
+    )
+    feeds = [pltpu.make_async_copy(a, b, feed.at[n]) for n, (a, b) in enumerate(inputs)]
+    for copy in feeds + loads:
         copy.start()
     barrier = pltpu.get_barrier_semaphore()
     for partner in partners:
@@ -155,8 +164,16 @@
 
     quarter = BI // NX
 
-    def piece(n, count):
-        return pl.ds(pl.multiple_of(n * count, 8), count)
+    feeds[0].wait()
+    feeds[1].wait()
+    lane = iota((8, 128), 1)
+    label_row = lane & 31
+    asks = jnp.zeros((8, 128), jnp.int32)
+    for s in range(NB):
+        label_row += jnp.where(lane >> 5 == s, (coords_ref[0, s] & (IB_DEV - 1)) * 32, 0)
+        asks += jnp.where(lane == s, coords_ref[1, s], 0) + jnp.where(lane == NB + s, coords_ref[2, s], 0)
+    level = iota((8, 128), 0)
+    info_ref[...] = jnp.where(level == 0, label_row, jnp.where(level == 1, asks, 0))
 
     wishes = [push(info_ref, infos.at[z], at_z(d)) for d in range(1, NZ)]
     tags = [push(info_ref, codes.at[x], at_x(d)) for d in range(1, NX)]
@@ -170,12 +187,15 @@
         plane, count = planes[n]
         return plane.at[pl.ds(pl.multiple_of(place * count, count), count)]
 
+    along_y, across = [], []
     for n, ref in ((0, fc_ref), (1, fb_ref)):
         plane, count = planes[n]
+        feeds[2 + n].wait()
         for k in range(count):
             plane[own * count + k] = ref[:, 128 * k : 128 * k + 128]
-    along_y = [[push(part(n, own), part(n, own), at_y(d)) for d in range(1, NY)] for n in range(2)]
-    across = [[push(part(n, own), part(n, own), at_c)] for n in range(2)]
+        along_y.append([push(part(n, own), part(n, own), at_y(d)) for d in (2, 1, 3)])
+        across.append([push(part(n, own), part(n, own), at_c)])
+    feeds[4].wait()
     space[...] = orthonormal_t(start_ref[...])
     for copy in wishes:
         copy.wait_recv()
@@ -184,8 +204,8 @@
     copy.wait()
 
     def relay(n):
-        for d in range(1, NY):
-            along_y[n][d - 1].wait_recv()
+        for k, d in ((1, 1), (2, 3), (0, 2)):
+            along_y[n][k].wait_recv()
             place = lax.rem(y + NY - d, NY) * 2 + c
             across[n].append(push(part(n, place), part(n, place), at_c))
         for copy in across[n]:
@@ -224,20 +244,16 @@
     for copy in sent_b:
         copy.wait_recv()
 
-    def contract_step(s, carry):
+    moves = []
+    for s in range(NB):
         alive = jnp.clip(counts_ref[0] - s, 0, 1).astype(F32)
         total = contract_slot(folded, s, got_b[(coords_ref[1, s] >> 7) * NB + s], alive)
         high = total.astype(BF16)
         high_ref[s] = high
+        for d in (2, 1, 3):
+            there = pl.ds(pl.multiple_of(lax.rem(x + d, NX) * quarter, quarter), quarter)
+            moves.append(push(high_ref.at[s, there, :], rows.at[x, s], at_x(d)))
         low_ref[s] = (total - high.astype(F32)).astype(BF16)
-        return carry
-
-    lax.fori_loop(0, NB, contract_step, 0)
-
-    moves = [
-        push(high_ref.at[:, pl.ds(pl.multiple_of(lax.rem(x + d, NX) * quarter, quarter), quarter), :], rows.at[x], at_x(d))
-        for d in range(1, NX)
-    ]
     rows[x] = high_ref[:, pl.ds(pl.multiple_of(x * quarter, quarter), quarter), :]
     for copy in tags:
         copy.wait_recv()
@@ -259,48 +275,71 @@
             g[pl.ds(128 * at, 128), :] = strip[:, 128 * n : 128 * n + 128]
             at += 1
 
-    base = c * HALF
-    copy = push(g.at[piece(1 - c, HALF)], from_c, at_c)
-    copy.wait_recv()
-    g[piece(c, HALF), :] += from_c[...]
-
-    copies = [
-        push(g.at[pl.ds(pl.multiple_of(base + lax.rem(x + d, NX) * PART_X, 8), PART_X)], from_x.at[d - 1], at_x(d))
-        for d in range(1, NX)
-    ]
-    for copy in copies:
-        copy.wait_recv()
-    base = base + x * PART_X
-    mine = pl.ds(pl.multiple_of(base, 8), PART_X)
-    g[mine, :] = g[mine, :] + from_x[0] + from_x[1] + from_x[2]
-
-    copies = [
-        push(g.at[pl.ds(pl.multiple_of(base + lax.rem(y + d, NY) * PART_Y, 8), PART_Y)], from_y.at[d - 1], at_y(d))
-        for d in range(1, NY)
-    ]
-    for copy in copies:
-        copy.wait_recv()
-    base = base + y * PART_Y
-    mine = pl.ds(pl.multiple_of(base, 8), PART_Y)
-    from_z[z] = g[mine, :] + from_y[0] + from_y[1] + from_y[2]
-
-    copies = [push(from_z.at[z], from_z.at[z], at_z(d)) for d in range(1, NZ)]
+    parts = ((0, PART_0, x, y, at_x, at_y, from_u0, from_v0), (PART_0, PART_1, y, x, at_y, at_x, from_u1, from_v1))
+
+    def span(start, count):
+        return pl.ds(pl.multiple_of(start, 8), count)
+
+    def chunk(n, core, d):
+        off, count, mu = parts[n][:3]
+        return span(core * HALF + off + lax.rem(mu + d, 4) * (count // 4), count // 4)
+
+    pieces = [(n, d) for d in (2, 1, 3, 0) for n in range(2)]
+    crossed = [push(g.at[chunk(n, 1 - c, d)], from_c.at[chunk(n, 0, d)], at_c) for n, d in pieces]
+    outgoing = [[], []]
+    for copy, (n, d) in zip(crossed, pieces):
+        copy.wait_recv()
+        here = chunk(n, c, d)
+        g[here, :] += from_c[chunk(n, 0, d), :]
+        if d > 0:
+            outgoing[n].append(push(g.at[here], parts[n][6].at[d - 1], parts[n][4](d)))
+
+    def small(n, d):
+        off, count, mu, mv = parts[n][:4]
+        return span(c * HALF + off + mu * (count // 4) + lax.rem(mv + d, 4) * (count // 16), count // 16)
+
+    second = [[], []]
+    for n in range(2):
+        for copy in outgoing[n]:
+            copy.wait_recv()
+        here = chunk(n, c, 0)
+        got = parts[n][6]
+        g[here, :] = g[here, :] + got[0] + got[1] + got[2]
+        second[n] = [push(g.at[small(n, d)], parts[n][7].at[d - 1], parts[n][5](d)) for d in (2, 1, 3)]
+    for n in range(2):
+        for copy in second[n]:
+            copy.wait_recv()
+        got = parts[n][7]
+        at = 0 if n == 0 else PART_0 // 16
+        from_z[z, at : at + parts[n][1] // 16, :] = g[small(n, 0), :] + got[0] + got[1] + got[2]
+    copies = [push(from_z.at[z], from_z.at[z], at_z(d)) for d in (4, 3, 5, 2, 6, 1, 7)]
     for copy in copies:
         copy.wait_recv()
     total = from_z[0]
     for n in range(1, NZ):
         total = total + from_z[n]
-    o[mine, :] = total
-
-    copies = [push(o.at[mine], o.at[mine], at_y(d)) for d in range(1, NY)]
-    for copy in copies:
-        copy.wait_recv()
-    mine = pl.ds(pl.multiple_of(c * HALF + x * PART_X, 8), PART_X)
-    copies = [push(o.at[mine], o.at[mine], at_x(d)) for d in range(1, NX)]
-    for copy in copies:
-        copy.wait_recv()
-    copy = push(o.at[piece(c, HALF)], o.at[piece(c, HALF)], at_c)
-    copy.wait_recv()
+
+    back = [[], []]
+    for n in range(2):
+        at = 0 if n == 0 else PART_0 // 16
+        here = small(n, 0)
+        o[here, :] = total[at : at + parts[n][1] // 16]
+        back[n] = [push(o.at[here], o.at[here], parts[n][5](d)) for d in (2, 1, 3)]
+    wide_back = [[], []]
+    relayed = []
+    for n in range(2):
+        for copy in back[n]:
+            copy.wait_recv()
+        here = chunk(n, c, 0)
+        wide_back[n] = [push(o.at[here], o.at[here], parts[n][4](d)) for d in (2, 1, 3)]
+        relayed.append(push(o.at[here], o.at[here], at_c))
+    for k, d in ((1, 1), (2, 3), (0, 2)):
+        for n in range(2):
+            wide_back[n][k].wait_recv()
+            here = chunk(n, c, 4 - d)
+            relayed.append(push(o.at[here], o.at[here], at_c))
+    for copy in relayed:
+        copy.wait_recv()
 
     for n, (p, q) in enumerate(TILES):
         tile = o[pl.ds(128 * n, 128), :]
@@ -322,11 +361,14 @@
     high = high_ref[...].reshape(RR, RR)
     low = low_ref[...].reshape(RR, RR)
     both = dot_nt(jnp.concatenate([wh, wm], axis=0), high)
-    maps[x] = both[:R2] + (both[R2:] + dot_nt(wh, low))
-    copies = [push(maps.at[x], maps.at[x], at_x(d)) for d in range(1, NX)]
+    mapped = both[:R2] + (both[R2:] + dot_nt(wh, low))
+    maps[x] = mapped
+    far[0] = mapped.astype(BF16)
+    copies = [push(far.at[0], far.at[d], at_x(d)) for d in range(1, NX)]
     first = (x * (IB_DEV // NX)).astype(F32)
-    for copy in copies:
-        copy.wait_recv()
+    for d in range(1, NX):
+        copies[d - 1].wait_recv()
+        maps[lax.rem(x + NX - d, NX)] = far[d].astype(F32)
     outs = [jnp.zeros((R2, BI), F32) for _ in range(IB_DEV // NX)]
     for n in range(NX):
         for s in range(NB):
@@ -340,17 +382,22 @@
         copy.wait_send()
 
 
-def factor(blocks, coords, counts, info, slab_b, slab_c, start_t):
-    copies = 65
+def factor(blocks, coords, counts, slab_b, slab_c, start_t):
+    copies = 100
     vmem = pl.BlockSpec(memory_space=pltpu.VMEM)
-    smem = pl.BlockSpec(memory_space=pltpu.SMEM)
     hbm = pl.BlockSpec(memory_space=pltpu.HBM)
     return pl.pallas_call(
         factor_kernel,
         out_shape=jax.ShapeDtypeStruct((R2, IB_DEV * BI // NX), F32),
-        in_specs=[hbm, smem, smem, vmem, vmem, vmem, vmem],
+        in_specs=[hbm] * 6,
         out_specs=vmem,
         scratch_shapes=[
+            pltpu.SMEM(coords.shape, jnp.int32),
+            pltpu.SMEM(counts.shape, jnp.int32),
+            pltpu.VMEM((8, 128), jnp.int32),
+            pltpu.VMEM(slab_b.shape, BF16),
+            pltpu.VMEM(slab_c.shape, BF16),
+            pltpu.VMEM(start_t.shape, F32),
             pltpu.VMEM((NB, BI, BJ * BK), BF16),
             pltpu.VMEM((2 * NY * 16, R2, BJ), BF16),
             pltpu.VMEM((2 * NY * 4, R3, 2 * BK), BF16),
@@ -368,30 +415,31 @@
             pltpu.VMEM((PACKED, 128), F32),
             pltpu.VMEM((PACKED, 128), F32),
             pltpu.VMEM((HALF, 128), F32),
-            pltpu.VMEM((NX - 1, PART_X, 128), F32),
-            pltpu.VMEM((NY - 1, PART_Y, 128), F32),
-            pltpu.VMEM((NZ, PART_Y, 128), F32),
+            pltpu.VMEM((3, PART_0 // 4, 128), F32),
+            pltpu.VMEM((3, PART_1 // 4, 128), F32),
+            pltpu.VMEM((3, PART_0 // 16, 128), F32),
+            pltpu.VMEM((3, PART_1 // 16, 128), F32),
+            pltpu.VMEM((NZ, HALF // 16, 128), F32),
             pltpu.VMEM((RR, RR), BF16),
             pltpu.VMEM((RR, RR), BF16),
             pltpu.VMEM((RR, RR), BF16),
             pltpu.VMEM((R2, RR), F32),
             pltpu.VMEM((NX, R2, RR), F32),
+            pltpu.VMEM((NX, R2, RR), BF16),
             pltpu.SemaphoreType.DMA((copies,)),
             pltpu.SemaphoreType.DMA((copies,)),
             pltpu.SemaphoreType.DMA((NB + 1,)),
+            pltpu.SemaphoreType.DMA((5,)),
         ],
         compiler_params=pltpu.CompilerParams(
-            collective_id=0, has_side_effects=True, vmem_limit_bytes=48 * 1024 * 1024
+            collective_id=0, has_side_effects=True, vmem_limit_bytes=60 * 1024 * 1024
         ),
         name="factor",
-    )(blocks, coords, counts, info, slab_b, slab_c, start_t)
+    )(blocks, coords, counts, slab_b, slab_c, start_t)
 
 
 def body(blocks, coords, counts, factor_b, factor_c, start):
-    code = ((coords[0] % IB_DEV)[:, None] * 32 + jnp.arange(32, dtype=jnp.int32)[None, :]).reshape(1, 128)
-    asks = jnp.pad(coords[1:].reshape(1, 2 * NB), ((0, 6), (0, 128 - 2 * NB)))
-    info = jnp.concatenate([code, asks], axis=0)
-    return factor(blocks, coords, counts, info, factor_b.T, factor_c.T, start.T).T
+    return factor(blocks, coords, counts, factor_b.T, factor_c.T, start.T).T
 
 
 def solution(mesh):

time: 106 us -> 84.9 us (0.80)
  Pallas kernels: 99.4 us -> 82.6 us
  local copies, waits for them, and re-layouts: 4.65 us -> 1.57 us
    pallas_call x1, Pallas kernels: 99.4 us -> 82.6 us  [factor(): pl.pallas_call(factor_kernel, out_shape=jax.ShapeDtypeStruct((R2, IB_DEV...]
    unnamed x9 -> x1, local copies, waits for them, and re-layouts: 3.8 us -> 1.57 us
where the time goes in v4:
time: 84.9 us; the launch traced here: 84.8 us
  Pallas kernels  82.6 us (97%)
  local copies, waits for them, and re-layouts  1.57 us (2%)
    pallas_call x1, Pallas kernels, factor(): pl.pallas_call(factor_kernel, out_shape=jax.ShapeDtypeStruct((R2, IB_DEV...  82.6 us

profile of v4, /device:TPU:1, one launch (start us, length us, event | category | flops | bytes accessed | tf_op | source)
XLA Modules:
  0.0 84.8 jit_solution(9790255313936300419)
XLA Ops:
  0.7 82.6 %factor.1 = f32[32,1024]{1,0:T(8,128)} custom-call(bf16[4,128,8192]{2,1,0:T(8,128)(2,1)} %blocks_ref.1, s32[3,4]{1,0:T(4,128)} %coords_hbm.1, s32[1]{0:T(128)S(6)} %copy.8.counts_hbm, bf16[32,2048]{1,0:T(8,128)(2,1)} %bitcast.5, bf16[16,512]{1,0:T(8,128)(2,1)} %bitcast.7, f32[32,512]{1,0:T(8,128)} %bitcast.6), custom_call_target="tpu_custom_call" | custom-call | tf_op jit(solution)/shard_map/factor/pallas_call | solution.py:389
  83.3 1.6 %copy.9 = f32[1024,32]{0,1:T(8,128)} copy(f32[1024,32]{0,1:T(8,128)} %bitcast.4) | data formatting | bytes 262144

commit v5 on v4

--- a/solution.py
+++ b/solution.py
@@ -40,26 +40,28 @@
 
 def fold_slot(held_x, slot, pair, odd, folded):
     pair = pair.astype(F32)
-    mode_c = pair[:, :BK] * (1.0 - odd) + pair[:, BK:] * odd
-    wide = jnp.concatenate([mode_c] * 8, axis=1)
-    tall = jnp.concatenate([wide] * 8, axis=0)
-    fold_mask = iota((128, 512), 0) // R3 == iota((128, 512), 1) // BK
-    fold_t = jnp.where(fold_mask, tall, 0.0).astype(BF16)
-    for t in range(16):
-        part = dot_nt(held_x[slot, :, 512 * t : 512 * t + 512], fold_t)
-        folded[slot, :, 128 * t : 128 * t + 128] = part.astype(BF16)
+    mode_c = (pair[:, :BK] * (1.0 - odd) + pair[:, BK:] * odd).astype(BF16)
+    spread = (iota((128, R3), 0) // 8 == iota((128, R3), 1)).astype(F32).astype(BF16)
+    tall = jnp.dot(spread, mode_c, preferred_element_type=F32)
+    wide = jnp.concatenate([tall] * 8, axis=1)
+    fold_mask = iota((128, 512), 0) % 8 == iota((128, 512), 1) // BK
+    fold_t = jnp.where(fold_mask, wide, 0.0).astype(BF16)
+    for t in range(8):
+        halves = [dot_nt(fold_t, held_x[slot, :, 512 * h : 512 * h + 512]) for h in (2 * t, 2 * t + 1)]
+        part = jnp.concatenate([half.reshape(R3, 8, BI) for half in halves], axis=1)
+        folded[slot, :, 16 * t : 16 * t + 16, :] = part.astype(BF16)
 
 
 def contract_slot(folded, slot, block_b, alive):
-    spread_q = (iota((RR, R2), 0) // R3 == iota((RR, R2), 1)).astype(F32).astype(BF16)
-    mode_b = jnp.dot(spread_q, block_b, preferred_element_type=F32).astype(BF16)
-    keep = (iota((RR, 256), 0) % R3 == iota((RR, 256), 1) % R3).astype(F32)
-    total = jnp.zeros((BI, RR), F32)
-    for t in range(8):
-        spread_j = (iota((BJ, 256), 0) == 16 * t + iota((BJ, 256), 1) // R3).astype(F32).astype(BF16)
-        expanded = jnp.dot(mode_b, spread_j, preferred_element_type=F32) * keep
-        total += dot_nt(folded[slot, :, 256 * t : 256 * t + 256], expanded.astype(BF16))
-    return total * alive
+    none = jnp.zeros((R2, BJ), BF16)
+    two = jnp.concatenate(
+        [jnp.concatenate([block_b, none], axis=1), jnp.concatenate([none, block_b], axis=1)], axis=0
+    )
+    parts = [
+        jnp.dot(two, folded[slot, 2 * t : 2 * t + 2].reshape(2 * BJ, BI), preferred_element_type=F32)
+        for t in range(R3 // 2)
+    ]
+    return jnp.concatenate(parts, axis=0) * alive
 
 
 def split(value):
@@ -113,7 +115,7 @@
 def factor_kernel(
     blocks_ref, coords_hbm, counts_hbm, fb_hbm, fc_hbm, start_hbm, out_ref,
     coords_ref, counts_ref, info_ref, fb_ref, fc_ref, start_ref,
-    held_x, plane_b, plane_c, infos, asked, give_b, give_c, got_b, got_c, folded, high_ref, low_ref,
+    held_x, plane_b, plane_c, infos, asked, give_b, give_c, got_b, got_c, folded, high_ref, turned_high, turned_low,
     rows, codes, g, o, from_c, from_u0, from_u1, from_v0, from_v1, from_z, gh, gm, gl, space, maps, far, send, recv, load, feed,
 ):
     b = lax.axis_index("blk")
@@ -187,31 +189,50 @@
         plane, count = planes[n]
         return plane.at[pl.ds(pl.multiple_of(place * count, count), count)]
 
-    along_y, across = [], []
-    for n, ref in ((0, fc_ref), (1, fb_ref)):
-        plane, count = planes[n]
-        feeds[2 + n].wait()
-        for k in range(count):
-            plane[own * count + k] = ref[:, 128 * k : 128 * k + 128]
-        along_y.append([push(part(n, own), part(n, own), at_y(d)) for d in (2, 1, 3)])
-        across.append([push(part(n, own), part(n, own), at_c)])
+    def half(d, h):
+        place = lax.rem(y + d, NY) * 2 + c
+        return plane_b.at[pl.ds(pl.multiple_of(place * 16 + 8 * h, 8), 8)]
+
+    feeds[2].wait()
+    for k in range(4):
+        plane_c[own * 4 + k] = fc_ref[:, 128 * k : 128 * k + 128]
+    along_y = [push(part(0, own), part(0, own), at_y(d)) for d in (2, 1, 3)]
+    across_c = [push(part(0, own), part(0, own), at_c)]
+    feeds[3].wait()
+    for k in range(16):
+        plane_b[own * 16 + k] = fb_ref[:, 128 * k : 128 * k + 128]
+    hops = {}
+    for d, h in ((1, 0), (3, 1), (1, 1), (3, 0)):
+        hops[d, h] = push(half(0, h), half(0, h), at_y(d))
+    across_b = [push(part(1, own), part(1, own), at_c)]
     feeds[4].wait()
-    space[...] = orthonormal_t(start_ref[...])
+    order = (iota((RR, RR), 0) // R3 == iota((RR, RR), 1) % R2) & (iota((RR, RR), 0) % R3 == iota((RR, RR), 1) // R2)
+    order = order.astype(F32).astype(BF16)
+    moved = jnp.dot(jnp.concatenate(split(start_ref[...]), axis=0), order, preferred_element_type=F32)
+    space[...] = orthonormal_t(moved[:R2] + (moved[R2 : 2 * R2] + moved[2 * R2 :]))
+
+    def came(d, h):
+        hops[d, h].wait_recv()
+        here = half(4 - d, h)
+        if (d, h) in ((1, 0), (3, 1)):
+            hops[2, h] = push(here, here, at_y(d))
+        across_b.append(push(here, here, at_c))
+
+    came(1, 0)
+    came(3, 1)
     for copy in wishes:
         copy.wait_recv()
     copy = pltpu.make_async_copy(infos, asked, load.at[NB])
     copy.start()
     copy.wait()
 
-    def relay(n):
-        for k, d in ((1, 1), (2, 3), (0, 2)):
-            along_y[n][k].wait_recv()
-            place = lax.rem(y + NY - d, NY) * 2 + c
-            across[n].append(push(part(n, place), part(n, place), at_c))
-        for copy in across[n]:
-            copy.wait_recv()
-
-    relay(0)
+    for k, d in ((1, 1), (2, 3), (0, 2)):
+        along_y[k].wait_recv()
+        place = lax.rem(y + NY - d, NY) * 2 + c
+        across_c.append(push(part(0, place), part(0, place), at_c))
+    for copy in across_c:
+        copy.wait_recv()
+
     def answer(plane, mode, shift, mask, give, got):
         sent = []
         for d in range(NZ):
@@ -228,7 +249,10 @@
         return sent
 
     sent_c = answer(plane_c, 1, 1, 31, give_c, got_c)
-    relay(1)
+    for d, h in ((1, 1), (3, 0), (2, 0), (2, 1)):
+        came(d, h)
+    for copy in across_b:
+        copy.wait_recv()
     sent_b = answer(plane_b, 0, 0, 127, give_b, got_b)
     for copy in loads:
         copy.wait()
@@ -245,15 +269,19 @@
         copy.wait_recv()
 
     moves = []
+    unit = (iota((BI, BI), 0) == iota((BI, BI), 1)).astype(F32).astype(BF16)
     for s in range(NB):
         alive = jnp.clip(counts_ref[0] - s, 0, 1).astype(F32)
         total = contract_slot(folded, s, got_b[(coords_ref[1, s] >> 7) * NB + s], alive)
         high = total.astype(BF16)
-        high_ref[s] = high
+        for k in range(RR // 128):
+            turned = dot_nt(unit, high[128 * k : 128 * k + 128])
+            high_ref[s, :, 128 * k : 128 * k + 128] = turned.astype(BF16)
         for d in (2, 1, 3):
             there = pl.ds(pl.multiple_of(lax.rem(x + d, NX) * quarter, quarter), quarter)
             moves.append(push(high_ref.at[s, there, :], rows.at[x, s], at_x(d)))
-        low_ref[s] = (total - high.astype(F32)).astype(BF16)
+        turned_high[:, 128 * s : 128 * s + 128] = high
+        turned_low[:, 128 * s : 128 * s + 128] = (total - high.astype(F32)).astype(BF16)
     rows[x] = high_ref[:, pl.ds(pl.multiple_of(x * quarter, quarter), quarter), :]
     for copy in tags:
         copy.wait_recv()
@@ -358,10 +386,8 @@
     small = inner_product(last, fine_dot(last, gh[...], gm[...], gl[...]))
     wide = fine_dot(inverse_lower(small), *split(last))
     wh, wm, _ = split(wide)
-    high = high_ref[...].reshape(RR, RR)
-    low = low_ref[...].reshape(RR, RR)
-    both = dot_nt(jnp.concatenate([wh, wm], axis=0), high)
-    mapped = both[:R2] + (both[R2:] + dot_nt(wh, low))
+    both = jnp.dot(jnp.concatenate([wh, wm], axis=0), turned_high[...], preferred_element_type=F32)
+    mapped = both[:R2] + (both[R2:] + jnp.dot(wh, turned_low[...], preferred_element_type=F32))
     maps[x] = mapped
     far[0] = mapped.astype(BF16)
     copies = [push(far.at[0], far.at[d], at_x(d)) for d in range(1, NX)]
@@ -383,7 +409,7 @@
 
 
 def factor(blocks, coords, counts, slab_b, slab_c, start_t):
-    copies = 100
+    copies = 110
     vmem = pl.BlockSpec(memory_space=pltpu.VMEM)
     hbm = pl.BlockSpec(memory_space=pltpu.HBM)
     return pl.pallas_call(
@@ -407,9 +433,10 @@
             pltpu.VMEM((NZ - 1, NB, R3, 2 * BK), BF16),
             pltpu.VMEM((NZ * NB, R2, BJ), BF16),
             pltpu.VMEM((NZ * NB, R3, 2 * BK), BF16),
-            pltpu.VMEM((NB, BI, BJ * R3), BF16),
+            pltpu.VMEM((NB, R3, BJ, BI), BF16),
             pltpu.VMEM((NB, BI, RR), BF16),
-            pltpu.VMEM((NB, BI, RR), BF16),
+            pltpu.VMEM((RR, NB * BI), BF16),
+            pltpu.VMEM((RR, NB * BI), BF16),
             pltpu.VMEM((NX, NB, BI // NX, RR), BF16),
             pltpu.VMEM((NX, 8, 128), jnp.int32),
             pltpu.VMEM((PACKED, 128), F32),

time: 84.9 us -> 80.7 us (0.951)
  Pallas kernels: 82.6 us -> 78.3 us
    pallas_call x1, Pallas kernels: 82.6 us -> 78.3 us  [factor(): pl.pallas_call(factor_kernel, out_shape=jax.ShapeDtypeStruct((R2, IB_DEV...]
where the time goes in v5:
time: 80.7 us; the launch traced here: 80.6 us
  Pallas kernels  78.3 us (97%)
  local copies, waits for them, and re-layouts  1.57 us (2%)
    pallas_call x1, Pallas kernels, factor(): pl.pallas_call(factor_kernel, out_shape=jax.ShapeDtypeStruct((R2, IB_DEV...  78.3 us

profile of v5, /device:TPU:1, one launch (start us, length us, event | category | flops | bytes accessed | tf_op | source)
XLA Modules:
  0.0 80.6 jit_solution(1493909555157032525)
XLA Ops:
  0.7 78.3 %factor.1 = f32[32,1024]{1,0:T(8,128)} custom-call(bf16[4,128,8192]{2,1,0:T(8,128)(2,1)} %blocks_ref.1, s32[3,4]{1,0:T(4,128)} %coords_hbm.1, s32[1]{0:T(128)S(6)} %copy.8.counts_hbm, bf16[32,2048]{1,0:T(8,128)(2,1)} %bitcast.5, bf16[16,512]{1,0:T(8,128)(2,1)} %bitcast.7, f32[32,512]{1,0:T(8,128)} %bitcast.6), custom_call_target="tpu_custom_call" | custom-call | tf_op jit(solution)/shard_map/factor/pallas_call | solution.py:415
  79.0 1.6 %copy.9 = f32[1024,32]{0,1:T(8,128)} copy(f32[1024,32]{0,1:T(8,128)} %bitcast.4) | data formatting | bytes 262144

commit v6 on v5

--- a/solution.py
+++ b/solution.py
@@ -146,7 +146,6 @@
     barrier = pltpu.get_barrier_semaphore()
     for partner in partners:
         pl.semaphore_signal(barrier, inc=1, device_id=partner, device_id_type=pl.DeviceIdType.MESH)
-    pl.semaphore_wait(barrier, len(partners))
 
     started = []
 
@@ -177,12 +176,20 @@
     level = iota((8, 128), 0)
     info_ref[...] = jnp.where(level == 0, label_row, jnp.where(level == 1, asks, 0))
 
+    infos[z] = info_ref[...]
+    codes[x] = info_ref[...]
+    own = y * 2 + c
+    feeds[2].wait()
+    for k in range(4):
+        plane_c[own * 4 + k] = fc_ref[:, 128 * k : 128 * k + 128]
+    feeds[3].wait()
+    for k in range(16):
+        plane_b[own * 16 + k] = fb_ref[:, 128 * k : 128 * k + 128]
+    pl.semaphore_wait(barrier, len(partners))
+
     wishes = [push(info_ref, infos.at[z], at_z(d)) for d in range(1, NZ)]
     tags = [push(info_ref, codes.at[x], at_x(d)) for d in range(1, NX)]
-    infos[z] = info_ref[...]
-    codes[x] = info_ref[...]
-
-    own = y * 2 + c
+
     planes = ((plane_c, 4), (plane_b, 16))
 
     def part(n, place):
@@ -193,24 +200,12 @@
         place = lax.rem(y + d, NY) * 2 + c
         return plane_b.at[pl.ds(pl.multiple_of(place * 16 + 8 * h, 8), 8)]
 
-    feeds[2].wait()
-    for k in range(4):
-        plane_c[own * 4 + k] = fc_ref[:, 128 * k : 128 * k + 128]
     along_y = [push(part(0, own), part(0, own), at_y(d)) for d in (2, 1, 3)]
     across_c = [push(part(0, own), part(0, own), at_c)]
-    feeds[3].wait()
-    for k in range(16):
-        plane_b[own * 16 + k] = fb_ref[:, 128 * k : 128 * k + 128]
     hops = {}
     for d, h in ((1, 0), (3, 1), (1, 1), (3, 0)):
         hops[d, h] = push(half(0, h), half(0, h), at_y(d))
     across_b = [push(part(1, own), part(1, own), at_c)]
-    feeds[4].wait()
-    order = (iota((RR, RR), 0) // R3 == iota((RR, RR), 1) % R2) & (iota((RR, RR), 0) % R3 == iota((RR, RR), 1) // R2)
-    order = order.astype(F32).astype(BF16)
-    moved = jnp.dot(jnp.concatenate(split(start_ref[...]), axis=0), order, preferred_element_type=F32)
-    space[...] = orthonormal_t(moved[:R2] + (moved[R2 : 2 * R2] + moved[2 * R2 :]))
-
     def came(d, h):
         hops[d, h].wait_recv()
         here = half(4 - d, h)
@@ -218,42 +213,52 @@
             hops[2, h] = push(here, here, at_y(d))
         across_b.append(push(here, here, at_c))
 
-    came(1, 0)
-    came(3, 1)
-    for copy in wishes:
-        copy.wait_recv()
-    copy = pltpu.make_async_copy(infos, asked, load.at[NB])
-    copy.start()
-    copy.wait()
-
     for k, d in ((1, 1), (2, 3), (0, 2)):
         along_y[k].wait_recv()
         place = lax.rem(y + NY - d, NY) * 2 + c
         across_c.append(push(part(0, place), part(0, place), at_c))
+    came(1, 0)
+    came(3, 1)
+    for copy in wishes:
+        copy.wait_recv()
+    copy = pltpu.make_async_copy(infos, asked, load.at[NB])
+    copy.start()
+    copy.wait()
     for copy in across_c:
         copy.wait_recv()
 
-    def answer(plane, mode, shift, mask, give, got):
+    def answer(pick, count, give, got):
         sent = []
-        for d in range(NZ):
+        for d in (0, 4, 3, 5, 2, 6, 1, 7):
             t = lax.rem(z + d, NZ)
-            for s in range(NB):
-                block = plane[(asked[t, 1, NB * mode + s] >> shift) & mask]
+            for s in range(count):
                 if d == 0:
-                    got[z * NB + s] = block
+                    got[z * count + s] = pick(t, s)
                 else:
-                    give[d - 1, s] = block
+                    give[d - 1, s] = pick(t, s)
             if d > 0:
-                target = got.at[pl.ds(pl.multiple_of(z * NB, NB), NB)]
-                sent.append(push(give.at[d - 1], target, at_z(d)))
-        return sent
-
-    sent_c = answer(plane_c, 1, 1, 31, give_c, got_c)
+                target = got.at[pl.ds(pl.multiple_of(z * count, count), count)]
+                sent.append((d, push(give.at[d - 1], target, at_z(d))))
+        return [copy for _, copy in sorted(sent, key=lambda item: item[0])]
+
+    left_half = iota((R3, 2 * BK), 1) < BK
+
+    def half_c(t, s):
+        picked = []
+        for n in range(2):
+            wish = asked[t, 1, NB + 2 * s + n]
+            pair = plane_c[(wish >> 1) & 31].astype(F32)
+            swapped = jnp.concatenate([pair[:, BK:], pair[:, :BK]], axis=1)
+            move = ((wish & 1) ^ n).astype(F32)
+            picked.append(pair * (1.0 - move) + swapped * move)
+        return jnp.where(left_half, picked[0], picked[1]).astype(BF16)
+
+    sent_c = answer(half_c, NB // 2, give_c, got_c)
     for d, h in ((1, 1), (3, 0), (2, 0), (2, 1)):
         came(d, h)
     for copy in across_b:
         copy.wait_recv()
-    sent_b = answer(plane_b, 0, 0, 127, give_b, got_b)
+    sent_b = answer(lambda t, s: plane_b[asked[t, 1, s] & 127], NB, give_b, got_b)
     for copy in loads:
         copy.wait()
     for copy in sent_c:
@@ -261,7 +266,7 @@
 
     def fold_step(s, carry):
         wish = coords_ref[2, s]
-        fold_slot(held_x, s, got_c[(wish >> 6) * NB + s], (wish & 1).astype(F32), folded)
+        fold_slot(held_x, s, got_c[(wish >> 6) * (NB // 2) + (s >> 1)], (s & 1).astype(F32), folded)
         return carry
 
     lax.fori_loop(0, NB, fold_step, 0)
@@ -282,6 +287,12 @@
             moves.append(push(high_ref.at[s, there, :], rows.at[x, s], at_x(d)))
         turned_high[:, 128 * s : 128 * s + 128] = high
         turned_low[:, 128 * s : 128 * s + 128] = (total - high.astype(F32)).astype(BF16)
+    feeds[4].wait()
+    order = (iota((RR, RR), 0) // R3 == iota((RR, RR), 1) % R2) & (iota((RR, RR), 0) % R3 == iota((RR, RR), 1) // R2)
+    order = order.astype(F32).astype(BF16)
+    moved = jnp.dot(jnp.concatenate(split(start_ref[...]), axis=0), order, preferred_element_type=F32)
+    space[...] = orthonormal_t(moved[:R2] + (moved[R2 : 2 * R2] + moved[2 * R2 :]))
+
     rows[x] = high_ref[:, pl.ds(pl.multiple_of(x * quarter, quarter), quarter), :]
     for copy in tags:
         copy.wait_recv()
@@ -384,10 +395,10 @@
     lax.fori_loop(0, ITERS, step, 0)
     last = space[...]
     small = inner_product(last, fine_dot(last, gh[...], gm[...], gl[...]))
-    wide = fine_dot(inverse_lower(small), *split(last))
-    wh, wm, _ = split(wide)
+    wh, wm, _ = split(last)
     both = jnp.dot(jnp.concatenate([wh, wm], axis=0), turned_high[...], preferred_element_type=F32)
-    mapped = both[:R2] + (both[R2:] + jnp.dot(wh, turned_low[...], preferred_element_type=F32))
+    product = both[:R2] + (both[R2:] + jnp.dot(wh, turned_low[...], preferred_element_type=F32))
+    mapped = fine_dot(inverse_lower(small), *split(product))
     maps[x] = mapped
     far[0] = mapped.astype(BF16)
     copies = [push(far.at[0], far.at[d], at_x(d)) for d in range(1, NX)]
@@ -430,9 +441,9 @@
             pltpu.VMEM((NZ, 8, 128), jnp.int32),
             pltpu.SMEM((NZ, 8, 128), jnp.int32),
             pltpu.VMEM((NZ - 1, NB, R2, BJ), BF16),
-            pltpu.VMEM((NZ - 1, NB, R3, 2 * BK), BF16),
+            pltpu.VMEM((NZ - 1, NB // 2, R3, 2 * BK), BF16),
             pltpu.VMEM((NZ * NB, R2, BJ), BF16),
-            pltpu.VMEM((NZ * NB, R3, 2 * BK), BF16),
+            pltpu.VMEM((NZ * NB // 2, R3, 2 * BK), BF16),
             pltpu.VMEM((NB, R3, BJ, BI), BF16),
             pltpu.VMEM((NB, BI, RR), BF16),
             pltpu.VMEM((RR, NB * BI), BF16),

time: 80.7 us -> 79.2 us (0.981)
  Pallas kernels: 78.3 us -> 76.9 us
    pallas_call x1, Pallas kernels: 78.3 us -> 76.9 us  [factor(): pl.pallas_call(factor_kernel, out_shape=jax.ShapeDtypeStruct((R2, IB_DEV...]
where the time goes in v6:
time: 79.2 us; the launch traced here: 79.1 us
  Pallas kernels  76.9 us (97%)
  local copies, waits for them, and re-layouts  1.57 us (2%)
    pallas_call x1, Pallas kernels, factor(): pl.pallas_call(factor_kernel, out_shape=jax.ShapeDtypeStruct((R2, IB_DEV...  76.9 us

profile of v6, /device:TPU:1, one launch (start us, length us, event | category | flops | bytes accessed | tf_op | source)
XLA Modules:
  0.0 79.1 jit_solution(1015218080867751322)
XLA Ops:
  0.7 76.9 %factor.1 = f32[32,1024]{1,0:T(8,128)} custom-call(bf16[4,128,8192]{2,1,0:T(8,128)(2,1)} %blocks_ref.1, s32[3,4]{1,0:T(4,128)} %coords_hbm.1, s32[1]{0:T(128)S(6)} %copy.8.counts_hbm, bf16[32,2048]{1,0:T(8,128)(2,1)} %bitcast.5, bf16[16,512]{1,0:T(8,128)(2,1)} %bitcast.7, f32[32,512]{1,0:T(8,128)} %bitcast.6), custom_call_target="tpu_custom_call" | custom-call | tf_op jit(solution)/shard_map/factor/pallas_call | solution.py:426
  77.5 1.6 %copy.9 = f32[1024,32]{0,1:T(8,128)} copy(f32[1024,32]{0,1:T(8,128)} %bitcast.4) | data formatting | bytes 262144

commit v7 on v6

--- a/solution.py
+++ b/solution.py
@@ -1,3 +1,5 @@
+import functools
+
 import jax
 import jax.numpy as jnp
 from jax import lax
@@ -115,7 +117,7 @@
 def factor_kernel(
     blocks_ref, coords_hbm, counts_hbm, fb_hbm, fc_hbm, start_hbm, out_ref,
     coords_ref, counts_ref, info_ref, fb_ref, fc_ref, start_ref,
-    held_x, plane_b, plane_c, infos, asked, give_b, give_c, got_b, got_c, folded, high_ref, turned_high, turned_low,
+    held_x, plane_b, plane_c, infos, asked, give_b, give_c, got_b, got_c, folded, high_ref, turned_high, turned_low, via,
     rows, codes, g, o, from_c, from_u0, from_u1, from_v0, from_v1, from_z, gh, gm, gl, space, maps, far, send, recv, load, feed,
 ):
     b = lax.axis_index("blk")
@@ -273,7 +275,14 @@
     for copy in sent_b:
         copy.wait_recv()
 
-    moves = []
+    moves, staged = [], []
+
+    def forward(s):
+        for k in range(2):
+            staged[s][k].wait_recv()
+            origin = lax.rem(x + 3 - 2 * k, NX)
+            moves.append(push(via.at[k, s], rows.at[origin, s, pl.ds(16 * k, 16), :], at_x(2 * k + 1)))
+
     unit = (iota((BI, BI), 0) == iota((BI, BI), 1)).astype(F32).astype(BF16)
     for s in range(NB):
         alive = jnp.clip(counts_ref[0] - s, 0, 1).astype(F32)
@@ -282,17 +291,17 @@
         for k in range(RR // 128):
             turned = dot_nt(unit, high[128 * k : 128 * k + 128])
             high_ref[s, :, 128 * k : 128 * k + 128] = turned.astype(BF16)
-        for d in (2, 1, 3):
+        ends = [pl.ds(pl.multiple_of(lax.rem(x + 2, NX) * quarter + 16 * k, 16), 16) for k in range(2)]
+        staged.append([push(high_ref.at[s, ends[k], :], via.at[k, s], at_x(2 * k + 1)) for k in range(2)])
+        for d in (1, 3):
             there = pl.ds(pl.multiple_of(lax.rem(x + d, NX) * quarter, quarter), quarter)
             moves.append(push(high_ref.at[s, there, :], rows.at[x, s], at_x(d)))
+        if s > 1:
+            forward(s - 2)
         turned_high[:, 128 * s : 128 * s + 128] = high
         turned_low[:, 128 * s : 128 * s + 128] = (total - high.astype(F32)).astype(BF16)
-    feeds[4].wait()
-    order = (iota((RR, RR), 0) // R3 == iota((RR, RR), 1) % R2) & (iota((RR, RR), 0) % R3 == iota((RR, RR), 1) // R2)
-    order = order.astype(F32).astype(BF16)
-    moved = jnp.dot(jnp.concatenate(split(start_ref[...]), axis=0), order, preferred_element_type=F32)
-    space[...] = orthonormal_t(moved[:R2] + (moved[R2 : 2 * R2] + moved[2 * R2 :]))
-
+    forward(NB - 2)
+    forward(NB - 1)
     rows[x] = high_ref[:, pl.ds(pl.multiple_of(x * quarter, quarter), quarter), :]
     for copy in tags:
         copy.wait_recv()
@@ -352,6 +361,12 @@
         at = 0 if n == 0 else PART_0 // 16
         from_z[z, at : at + parts[n][1] // 16, :] = g[small(n, 0), :] + got[0] + got[1] + got[2]
     copies = [push(from_z.at[z], from_z.at[z], at_z(d)) for d in (4, 3, 5, 2, 6, 1, 7)]
+    feeds[4].wait()
+    order = (iota((RR, RR), 0) // R3 == iota((RR, RR), 1) % R2) & (iota((RR, RR), 0) % R3 == iota((RR, RR), 1) // R2)
+    order = order.astype(F32).astype(BF16)
+    moved = jnp.dot(jnp.concatenate(split(start_ref[...]), axis=0), order, preferred_element_type=F32)
+    space[...] = orthonormal_t(moved[:R2] + (moved[R2 : 2 * R2] + moved[2 * R2 :]))
+
     for copy in copies:
         copy.wait_recv()
     total = from_z[0]
@@ -420,7 +435,7 @@
 
 
 def factor(blocks, coords, counts, slab_b, slab_c, start_t):
-    copies = 110
+    copies = 120
     vmem = pl.BlockSpec(memory_space=pltpu.VMEM)
     hbm = pl.BlockSpec(memory_space=pltpu.HBM)
     return pl.pallas_call(
@@ -448,6 +463,7 @@
             pltpu.VMEM((NB, BI, RR), BF16),
             pltpu.VMEM((RR, NB * BI), BF16),
             pltpu.VMEM((RR, NB * BI), BF16),
+            pltpu.VMEM((2, NB, 16, RR), BF16),
             pltpu.VMEM((NX, NB, BI // NX, RR), BF16),
             pltpu.VMEM((NX, 8, 128), jnp.int32),
             pltpu.VMEM((PACKED, 128), F32),
@@ -470,14 +486,15 @@
             pltpu.SemaphoreType.DMA((5,)),
         ],
         compiler_params=pltpu.CompilerParams(
-            collective_id=0, has_side_effects=True, vmem_limit_bytes=60 * 1024 * 1024
+            collective_id=0, has_side_effects=True, vmem_limit_bytes=53 * 1024 * 1024
         ),
         name="factor",
     )(blocks, coords, counts, slab_b, slab_c, start_t)
 
 
 def body(blocks, coords, counts, factor_b, factor_c, start):
-    return factor(blocks, coords, counts, factor_b.T, factor_c.T, start.T).T
+    hold = functools.partial(pltpu.with_memory_space_constraint, memory_space=pltpu.HBM)
+    return factor(blocks, hold(coords), counts, hold(factor_b.T), hold(factor_c.T), hold(start.T)).T
 
 
 def solution(mesh):

time: 79.2 us -> 79.1 us (level)
  local copies, waits for them, and re-layouts: 1.57 us -> 0.66 us
  Pallas kernels: 76.9 us -> 77.7 us
    unnamed x1, local copies, waits for them, and re-layouts: 1.57 us -> 0.66 us
    pallas_call x1, Pallas kernels: 76.9 us -> 77.7 us  [factor(): pl.pallas_call(factor_kernel, out_shape=jax.ShapeDtypeStruct((R2, IB_DEV...]
where the time goes in v7:
time: 79.1 us; the launch traced here: 79 us
  Pallas kernels  77.7 us (98%)
    pallas_call x1, Pallas kernels, factor(): pl.pallas_call(factor_kernel, out_shape=jax.ShapeDtypeStruct((R2, IB_DEV...  77.7 us

profile of v7, /device:TPU:1, one launch (start us, length us, event | category | flops | bytes accessed | tf_op | source)
XLA Modules:
  0.0 79.0 jit_solution(5811246933284418106)
XLA Ops:
  0.7 77.7 %factor.1 = f32[32,1024]{1,0:T(8,128)S(1)} custom-call(bf16[4,128,8192]{2,1,0:T(8,128)(2,1)} %blocks_ref.1, s32[3,4]{1,0:T(4,128)} %coords_hbm.1, s32[1]{0:T(128)S(6)} %copy.8.counts_hbm, bf16[32,2048]{1,0:T(8,128)(2,1)} %bitcast.5, bf16[16,512]{1,0:T(8,128)(2,1)} %bitcast.7, f32[32,512]{1,0:T(8,128)} %bitcast.6), custom_call_target="tpu_custom_call" | custom-call | tf_op jit(solution)/shard_map/factor/pallas_call | solution.py:441
  78.3 0.7 copy.9

commit v8 on v7

--- a/solution.py
+++ b/solution.py
@@ -117,7 +117,7 @@
 def factor_kernel(
     blocks_ref, coords_hbm, counts_hbm, fb_hbm, fc_hbm, start_hbm, out_ref,
     coords_ref, counts_ref, info_ref, fb_ref, fc_ref, start_ref,
-    held_x, plane_b, plane_c, infos, asked, give_b, give_c, got_b, got_c, folded, high_ref, turned_high, turned_low, via,
+    held_x, plane_b, plane_c, infos, asked, give_b, give_c, got_b, got_c, folded, high_ref, turned_high, turned_low,
     rows, codes, g, o, from_c, from_u0, from_u1, from_v0, from_v1, from_z, gh, gm, gl, space, maps, far, send, recv, load, feed,
 ):
     b = lax.axis_index("blk")
@@ -275,13 +275,7 @@
     for copy in sent_b:
         copy.wait_recv()
 
-    moves, staged = [], []
-
-    def forward(s):
-        for k in range(2):
-            staged[s][k].wait_recv()
-            origin = lax.rem(x + 3 - 2 * k, NX)
-            moves.append(push(via.at[k, s], rows.at[origin, s, pl.ds(16 * k, 16), :], at_x(2 * k + 1)))
+    moves = []
 
     unit = (iota((BI, BI), 0) == iota((BI, BI), 1)).astype(F32).astype(BF16)
     for s in range(NB):
@@ -291,17 +285,11 @@
         for k in range(RR // 128):
             turned = dot_nt(unit, high[128 * k : 128 * k + 128])
             high_ref[s, :, 128 * k : 128 * k + 128] = turned.astype(BF16)
-        ends = [pl.ds(pl.multiple_of(lax.rem(x + 2, NX) * quarter + 16 * k, 16), 16) for k in range(2)]
-        staged.append([push(high_ref.at[s, ends[k], :], via.at[k, s], at_x(2 * k + 1)) for k in range(2)])
-        for d in (1, 3):
+        for d in (2, 1, 3):
             there = pl.ds(pl.multiple_of(lax.rem(x + d, NX) * quarter, quarter), quarter)
             moves.append(push(high_ref.at[s, there, :], rows.at[x, s], at_x(d)))
-        if s > 1:
-            forward(s - 2)
         turned_high[:, 128 * s : 128 * s + 128] = high
         turned_low[:, 128 * s : 128 * s + 128] = (total - high.astype(F32)).astype(BF16)
-    forward(NB - 2)
-    forward(NB - 1)
     rows[x] = high_ref[:, pl.ds(pl.multiple_of(x * quarter, quarter), quarter), :]
     for copy in tags:
         copy.wait_recv()
@@ -354,30 +342,34 @@
         got = parts[n][6]
         g[here, :] = g[here, :] + got[0] + got[1] + got[2]
         second[n] = [push(g.at[small(n, d)], parts[n][7].at[d - 1], parts[n][5](d)) for d in (2, 1, 3)]
+    summed_z = [[], []]
     for n in range(2):
         for copy in second[n]:
             copy.wait_recv()
         got = parts[n][7]
         at = 0 if n == 0 else PART_0 // 16
-        from_z[z, at : at + parts[n][1] // 16, :] = g[small(n, 0), :] + got[0] + got[1] + got[2]
-    copies = [push(from_z.at[z], from_z.at[z], at_z(d)) for d in (4, 3, 5, 2, 6, 1, 7)]
+        lines = slice(at, at + parts[n][1] // 16)
+        from_z[z, lines, :] = g[small(n, 0), :] + got[0] + got[1] + got[2]
+        place = from_z.at[z, lines]
+        summed_z[n] = [push(place, place, at_z(d)) for d in (4, 3, 5, 2, 6, 1, 7)]
     feeds[4].wait()
     order = (iota((RR, RR), 0) // R3 == iota((RR, RR), 1) % R2) & (iota((RR, RR), 0) % R3 == iota((RR, RR), 1) // R2)
     order = order.astype(F32).astype(BF16)
     moved = jnp.dot(jnp.concatenate(split(start_ref[...]), axis=0), order, preferred_element_type=F32)
     space[...] = orthonormal_t(moved[:R2] + (moved[R2 : 2 * R2] + moved[2 * R2 :]))
 
-    for copy in copies:
-        copy.wait_recv()
-    total = from_z[0]
-    for n in range(1, NZ):
-        total = total + from_z[n]
 
     back = [[], []]
     for n in range(2):
         at = 0 if n == 0 else PART_0 // 16
         here = small(n, 0)
-        o[here, :] = total[at : at + parts[n][1] // 16]
+        for copy in summed_z[n]:
+            copy.wait_recv()
+        lines = slice(at, at + parts[n][1] // 16)
+        total = from_z[0, lines]
+        for k in range(1, NZ):
+            total = total + from_z[k, lines]
+        o[here, :] = total
         back[n] = [push(o.at[here], o.at[here], parts[n][5](d)) for d in (2, 1, 3)]
     wide_back = [[], []]
     relayed = []
@@ -463,7 +455,6 @@
             pltpu.VMEM((NB, BI, RR), BF16),
             pltpu.VMEM((RR, NB * BI), BF16),
             pltpu.VMEM((RR, NB * BI), BF16),
-            pltpu.VMEM((2, NB, 16, RR), BF16),
             pltpu.VMEM((NX, NB, BI // NX, RR), BF16),
             pltpu.VMEM((NX, 8, 128), jnp.int32),
             pltpu.VMEM((PACKED, 128), F32),

time: 79.1 us -> 78.1 us (0.987)
  Pallas kernels: 77.7 us -> 76.7 us
    pallas_call x1, Pallas kernels: 77.7 us -> 76.7 us  [factor(): pl.pallas_call(factor_kernel, out_shape=jax.ShapeDtypeStruct((R2, IB_DEV...]
where the time goes in v8:
time: 78.1 us
  Pallas kernels  76.7 us (98%)
    pallas_call x1, Pallas kernels, factor(): pl.pallas_call(factor_kernel, out_shape=jax.ShapeDtypeStruct((R2, IB_DEV...  76.7 us

profile of v8, /device:TPU:1, one launch (start us, length us, event | category | flops | bytes accessed | tf_op | source)
XLA Modules:
  0.0 78.1 jit_solution(18224162490706048793)
XLA Ops:
  0.7 76.7 %factor.1 = f32[32,1024]{1,0:T(8,128)S(1)} custom-call(bf16[4,128,8192]{2,1,0:T(8,128)(2,1)} %blocks_ref.1, s32[3,4]{1,0:T(4,128)} %coords_hbm.1, s32[1]{0:T(128)S(6)} %copy.8.counts_hbm, bf16[32,2048]{1,0:T(8,128)(2,1)} %bitcast.5, bf16[16,512]{1,0:T(8,128)(2,1)} %bitcast.7, f32[32,512]{1,0:T(8,128)} %bitcast.6), custom_call_target="tpu_custom_call" | custom-call | tf_op jit(solution)/shard_map/factor/pallas_call | solution.py:433
  77.4 0.7 copy.9

commit v9 on v8

--- a/solution.py
+++ b/solution.py
@@ -189,9 +189,6 @@
         plane_b[own * 16 + k] = fb_ref[:, 128 * k : 128 * k + 128]
     pl.semaphore_wait(barrier, len(partners))
 
-    wishes = [push(info_ref, infos.at[z], at_z(d)) for d in range(1, NZ)]
-    tags = [push(info_ref, codes.at[x], at_x(d)) for d in range(1, NX)]
-
     planes = ((plane_c, 4), (plane_b, 16))
 
     def part(n, place):
@@ -204,10 +201,13 @@
 
     along_y = [push(part(0, own), part(0, own), at_y(d)) for d in (2, 1, 3)]
     across_c = [push(part(0, own), part(0, own), at_c)]
+    wishes = [push(info_ref, infos.at[z], at_z(d)) for d in (4, 3, 5, 2, 6, 1, 7)]
     hops = {}
     for d, h in ((1, 0), (3, 1), (1, 1), (3, 0)):
         hops[d, h] = push(half(0, h), half(0, h), at_y(d))
     across_b = [push(part(1, own), part(1, own), at_c)]
+    tags = [push(info_ref, codes.at[x], at_x(d)) for d in range(1, NX)]
+
     def came(d, h):
         hops[d, h].wait_recv()
         here = half(4 - d, h)

time: 78.1 us -> 78.2 us (level)
  no operation moved by 1% of the time
where the time goes in v9:
time: 78.2 us; the launch traced here: 78.1 us
  Pallas kernels  76.8 us (98%)
    pallas_call x1, Pallas kernels, factor(): pl.pallas_call(factor_kernel, out_shape=jax.ShapeDtypeStruct((R2, IB_DEV...  76.8 us

profile of v9, /device:TPU:1, one launch (start us, length us, event | category | flops | bytes accessed | tf_op | source)
XLA Modules:
  0.0 78.1 jit_solution(7178691353697845271)
XLA Ops:
  0.7 76.8 %factor.1 = f32[32,1024]{1,0:T(8,128)S(1)} custom-call(bf16[4,128,8192]{2,1,0:T(8,128)(2,1)} %blocks_ref.1, s32[3,4]{1,0:T(4,128)} %coords_hbm.1, s32[1]{0:T(128)S(6)} %copy.8.counts_hbm, bf16[32,2048]{1,0:T(8,128)(2,1)} %bitcast.5, bf16[16,512]{1,0:T(8,128)(2,1)} %bitcast.7, f32[32,512]{1,0:T(8,128)} %bitcast.6), custom_call_target="tpu_custom_call" | custom-call | tf_op jit(solution)/shard_map/factor/pallas_call | solution.py:433
  77.5 0.7 copy.9

commit v10 on v9

--- a/solution.py
+++ b/solution.py
@@ -118,7 +118,7 @@
     blocks_ref, coords_hbm, counts_hbm, fb_hbm, fc_hbm, start_hbm, out_ref,
     coords_ref, counts_ref, info_ref, fb_ref, fc_ref, start_ref,
     held_x, plane_b, plane_c, infos, asked, give_b, give_c, got_b, got_c, folded, high_ref, turned_high, turned_low,
-    rows, codes, g, o, from_c, from_u0, from_u1, from_v0, from_v1, from_z, gh, gm, gl, space, maps, far, send, recv, load, feed,
+    rows, codes, g, o, from_c, from_u0, from_u1, from_v0, from_v1, from_z, gh, gm, gl, space, maps, send, recv, load, feed,
 ):
     b = lax.axis_index("blk")
     x = lax.axis_index("rep")
@@ -401,18 +401,14 @@
 
     lax.fori_loop(0, ITERS, step, 0)
     last = space[...]
-    small = inner_product(last, fine_dot(last, gh[...], gm[...], gl[...]))
     wh, wm, _ = split(last)
     both = jnp.dot(jnp.concatenate([wh, wm], axis=0), turned_high[...], preferred_element_type=F32)
-    product = both[:R2] + (both[R2:] + jnp.dot(wh, turned_low[...], preferred_element_type=F32))
-    mapped = fine_dot(inverse_lower(small), *split(product))
-    maps[x] = mapped
-    far[0] = mapped.astype(BF16)
-    copies = [push(far.at[0], far.at[d], at_x(d)) for d in range(1, NX)]
+    maps[x] = both[:R2] + (both[R2:] + jnp.dot(wh, turned_low[...], preferred_element_type=F32))
+    copies = [push(maps.at[x], maps.at[x], at_x(d)) for d in (2, 1, 3)]
+    lower = inverse_lower(inner_product(last, fine_dot(last, gh[...], gm[...], gl[...])))
     first = (x * (IB_DEV // NX)).astype(F32)
-    for d in range(1, NX):
-        copies[d - 1].wait_recv()
-        maps[lax.rem(x + NX - d, NX)] = far[d].astype(F32)
+    for copy in copies:
+        copy.wait_recv()
     outs = [jnp.zeros((R2, BI), F32) for _ in range(IB_DEV // NX)]
     for n in range(NX):
         for s in range(NB):
@@ -420,8 +416,7 @@
             term = maps[n, :, 128 * s : 128 * s + 128]
             for k in range(IB_DEV // NX):
                 outs[k] = outs[k] + jnp.where(label == float(k), term, 0.0)
-    for k in range(IB_DEV // NX):
-        out_ref[:, 128 * k : 128 * k + 128] = outs[k]
+    out_ref[...] = fine_dot(lower, *split(jnp.concatenate(outs, axis=1)))
     for copy in started:
         copy.wait_send()
 
@@ -470,7 +465,6 @@
             pltpu.VMEM((RR, RR), BF16),
             pltpu.VMEM((R2, RR), F32),
             pltpu.VMEM((NX, R2, RR), F32),
-            pltpu.VMEM((NX, R2, RR), BF16),
             pltpu.SemaphoreType.DMA((copies,)),
             pltpu.SemaphoreType.DMA((copies,)),
             pltpu.SemaphoreType.DMA((NB + 1,)),

time: 78.2 us -> 78.1 us (level)
  no operation moved by 1% of the time
where the time goes in v10:
time: 78.1 us
  Pallas kernels  76.7 us (98%)
    pallas_call x1, Pallas kernels, factor(): pl.pallas_call(factor_kernel, out_shape=jax.ShapeDtypeStruct((R2, IB_DEV...  76.7 us

profile of v10, /device:TPU:1, one launch (start us, length us, event | category | flops | bytes accessed | tf_op | source)
XLA Modules:
  0.0 78.1 jit_solution(2982472477076125116)
XLA Ops:
  0.7 76.7 %factor.1 = f32[32,1024]{1,0:T(8,128)S(1)} custom-call(bf16[4,128,8192]{2,1,0:T(8,128)(2,1)} %blocks_ref.1, s32[3,4]{1,0:T(4,128)} %coords_hbm.1, s32[1]{0:T(128)S(6)} %copy.8.counts_hbm, bf16[32,2048]{1,0:T(8,128)(2,1)} %bitcast.5, bf16[16,512]{1,0:T(8,128)(2,1)} %bitcast.7, f32[32,512]{1,0:T(8,128)} %bitcast.6), custom_call_target="tpu_custom_call" | custom-call | tf_op jit(solution)/shard_map/factor/pallas_call | solution.py:428
  77.4 0.7 copy.9
